TPU v7x, 128 devices: a whole 4x4x4 slice. The times are simulated.
128 devices in a mesh: occ: 4 (over x), virt: 32 (over y, z, core).
Axes of the slice: x: 4, y: 4, z: 4, core: 2. Of those that a mesh axis runs over, the one named last changes fastest.
Arguments:
- amplitudes: bfloat16 [1, 100, 1024, 1024], P(None, 'occ', 'virt'), may hold values from -6 to 6
- cycle_block: bfloat16 [1024, 100, 4, 1024], P('virt', None, 'occ'), may hold values from -0.01953125 to 0.01953125
- drive_term: bfloat16 [1, 1024, 4, 1024], P(None, 'virt', 'occ'), may hold values from -6 to 6
- occ_energy: float32 [100], replicated, may hold values from -2 to -0.3
- virt_energy: float32 [1024], replicated, may hold values from 0.2 to 4
- occ_irrep: int32 [100], replicated, may hold values from 0 to 1
- virt_irrep: int32 [1024], replicated, may hold values from 0 to 1
- slab_occ: int32 [1], replicated, may hold values from 0 to 99
- col_occ: int32 [4], replicated, may hold values from 0 to 99
Outputs:
- amp_update: float32 [1, 1024, 4, 1024], P(None, 'virt', 'occ')
Inputs may be any that keep to these rules, and one draw needn't show every extreme that they name: `occ_irrep`: labels of the two irreducible representations of the C2 group. `virt_irrep`: labels of the two irreducible representations of the C2 group.
All inputs are finite; a program needn't handle non-finite values.
Results may differ from a plain program's by a relative error of at most 0.0003.
Values may be sent and summed in bfloat16 or wider, within the bound.
A program may use at most 64 MiB of HBM per device.

v0:
```python
import jax
import jax.numpy as jnp
from jax import lax
from jax.sharding import PartitionSpec as P


def pick_entries(values_table, indices):
    hits = indices[:, None] == jnp.arange(values_table.shape[0], dtype=jnp.int32)[None, :]
    return jnp.sum(
        jnp.where(hits, values_table[None, :], jnp.zeros((), values_table.dtype)), axis=1
    )


def body(
    amplitudes,
    cycle_block,
    drive_term,
    occ_energy,
    virt_energy,
    occ_irrep,
    virt_irrep,
    slab_occ,
    col_occ,
):
    k_rows = amplitudes.shape[1]
    a_cols = amplitudes.shape[2]
    j_cols = cycle_block.shape[2]
    occ_pos = lax.axis_index("occ")
    virt_pos = lax.axis_index("virt")
    slab_irrep = pick_entries(occ_irrep, slab_occ)
    col_irrep = pick_entries(occ_irrep, col_occ)
    irr_k = lax.dynamic_slice_in_dim(occ_irrep, occ_pos * k_rows, k_rows)
    irr_a = lax.dynamic_slice_in_dim(virt_irrep, virt_pos * a_cols, a_cols)
    parity = (
        slab_irrep[:, None, None, None]
        + irr_k[None, :, None, None]
        + irr_a[None, None, :, None]
        + virt_irrep[None, None, None, :]
    )
    masked = jnp.where(parity % 2 == 0, amplitudes, jnp.zeros((), amplitudes.dtype))
    pair_block = lax.all_gather(masked, "occ", axis=1, tiled=True)
    relaid = lax.all_to_all(pair_block, "virt", split_axis=3, concat_axis=2, tiled=True)
    partial_value = jnp.einsum(
        "skac,ckjb->sajb", relaid, cycle_block, preferred_element_type=jnp.float32
    )
    cycle_sum = lax.psum_scatter(partial_value, "virt", scatter_dimension=1, tiled=True)
    e_slab = pick_entries(occ_energy, slab_occ)
    e_cols = lax.dynamic_slice_in_dim(pick_entries(occ_energy, col_occ), occ_pos * j_cols, j_cols)
    irr_cols = lax.dynamic_slice_in_dim(col_irrep, occ_pos * j_cols, j_cols)
    e_rows = lax.dynamic_slice_in_dim(virt_energy, virt_pos * a_cols, a_cols)
    divisor = (
        e_rows[None, :, None, None]
        + virt_energy[None, None, None, :]
        - e_slab[:, None, None, None]
        - e_cols[None, None, :, None]
    )
    out_parity = (
        slab_irrep[:, None, None, None]
        + irr_a[None, :, None, None]
        + irr_cols[None, None, :, None]
        + virt_irrep[None, None, None, :]
    )
    value = (drive_term.astype(jnp.float32) + cycle_sum) / divisor
    return jnp.where(out_parity % 2 == 0, value, jnp.zeros((), jnp.float32))


def solution(mesh):
    in_specs = (
        P(None, "occ", "virt", None),
        P("virt", None, "occ", None),
        P(None, "virt", "occ", None),
        P(),
        P(),
        P(),
        P(),
        P(),
        P(),
    )
    out_specs = P(None, "virt", "occ", None)
    return jax.shard_map(body, mesh=mesh, in_specs=in_specs, out_specs=out_specs, check_vma=False)
```

profile of v0, /device:TPU:1, one launch (start us, length us, event | category | flops | bytes accessed | tf_op | source)
XLA Modules:
  0.0 337.6 jit_solution(3754829099605659137)
XLA Ops:
  6.5 0.0 all-gather.2.cloned.1.call-start
  7.2 1.4 fusion.10
  8.6 0.9 select_reduce_fusion.1
  9.4 1.4 dynamic-slice_add_fusion
  10.8 0.6 dynamic_slice.16
  11.4 2.1 add_add_fusion
  13.5 0.1 broadcast_add_fusion
  13.6 3.9 %fusion.4 = bf16[1,25,32,1024]{3,2,0,1:T(8,128)(2,1)} fusion(bf16[1,25,32,1024]{3,2,1,0:T(8,128)(2,1)} %param.9, s32[1024]{0:T(1024)} %param.15, s32[25,32]{1,0:T(8,128)S(1)} %broadcast_add_fusion), kind=kLoop, calls=%fused_computation.9 | loop fusion | flops 11468800 | bytes 3284096 | tf_op jit(solution)/shard_map/jit(_where)/select_n | solution.py:40
  17.4 0.0 all-gather.2.cloned.1.call-update
  17.5 0.0 reduce-scatter.2.cloned.1.call-start
  17.5 71.1 %all-gather.2.cloned.1.call-done = bf16[1,100,32,1024]{3,2,0,1:T(8,128)(2,1)} async-done(((bf16[1,25,32,1024]{3,2,0,1:T(8,128)(2,1)}), bf16[1,100,32,1024]{3,2,0,1:T(8,128)(2,1)}) %all-gather.2.cloned.1.call-update) | async-done | bytes 6553616 | tf_op jit(solution)/shard_map/all_gather | solution.py:41
  88.6 12.9 %copy.25 = bf16[1,100,32,1024]{1,2,0,3:T(8,128)(2,1)} copy(bf16[1,100,32,1024]{3,2,0,1:T(8,128)(2,1)} %all-gather.2.cloned.1.call-done) | data formatting | bytes 13107200 | tf_op jit(solution)/shard_map/all_gather | solution.py:41
  101.5 103.4 %all_to_all.15 = bf16[1,100,32,1024]{1,2,0,3:T(8,128)(2,1)} all-to-all(bf16[1,100,32,1024]{1,2,0,3:T(8,128)(2,1)} %copy.25), channel_id=1, replica_groups=mesh['occ'=4,'virt'=32] {'virt'}, dimensions={3} | all-to-all | bytes 13107200 | tf_op jit(solution)/shard_map/all_to_all | solution.py:42
  204.9 9.8 %copy.26 = bf16[1,100,32,1024]{1,3,2,0:T(8,128)(2,1)} copy(bf16[1,100,32,1024]{1,2,0,3:T(8,128)(2,1)} %all_to_all.15) | data formatting | bytes 13107200 | tf_op jit(solution)/shard_map/all_to_all | solution.py:42
  214.7 9.1 %copy.27 = bf16[1,100,32,32,32]{1,4,3,2,0:T(8,128)(2,1)} copy(bf16[1,100,32,32,32]{1,4,2,3,0:T(8,128)(2,1)} %bitcast.22) | data formatting | bytes 13107200 | tf_op jit(solution)/shard_map/all_to_all | solution.py:42
  223.9 13.4 %copy.28 = bf16[100,1024,32]{1,2,0:T(8,128)(2,1)} copy(bf16[100,1024,32]{0,2,1:T(8,128)(2,1)} %bitcast.21) | data formatting | bytes 13107200 | tf_op jit(solution)/shard_map/reshape.10
  237.2 12.7 %fusion.5 = f32[1,1024,1,1024]{3,1,2,0:T(8,128)} fusion(bf16[100,1024,32]{1,2,0:T(8,128)(2,1)} %copy.28, bf16[32,100,1,1024]{3,0,2,1:T(8,128)(2,1)} %param.10), kind=kOutput, calls=%fused_computation.10 | convolution fusion | flops 6710886400 | bytes 17301504 | tf_op jit(solution)/shard_map/skac,ckjb->sajb/dot_general | solution.py:43
  249.9 0.0 copy-start.3
  249.9 0.0 copy-start.4
  250.0 0.0 copy-start.2
  250.0 0.0 copy-start
  250.0 0.0 copy-start.1
  250.0 0.0 reduce-scatter.2.cloned.1.call-update
  250.0 0.6 copy-done.3
  250.6 0.0 copy-done.4
  250.6 0.2 select_reduce_fusion
  250.8 0.6 dynamic_slice.19
  251.4 0.0 copy-done.2
  251.4 0.1 dynamic_slice.18
  251.5 0.6 fusion.11
  252.1 75.5 %reduce-scatter.2.cloned.1.call-done = f32[1,32,1,1024]{3,1,2,0:T(8,128)} async-done(((f32[1,1024,1,1024]{3,1,2,0:T(8,128)}), f32[1,32,1,1024]{3,1,2,0:T(8,128)}) %reduce-scatter.2.cloned.1.call-update) | async-done | bytes 131088 | tf_op jit(solution)/shard_map/reduce_scatter | solution.py:46
  327.6 0.0 copy-done
  327.6 0.0 copy-done.1
  327.6 2.3 divide_select_fusion
  329.9 0.8 copy.29
Async XLA Ops:
  6.5 82.1 %all-gather.2.cloned.1.call-start = ((), (), s32[]{:S(2)}) async-start(), calls=%async_computation.2 | async-start | bytes 8192000 | tf_op jit(solution)/shard_map/all_gather | solution.py:41
  17.5 310.1 %reduce-scatter.2.cloned.1.call-start = ((), (), s32[]{:S(2)}) async-start(), calls=%async_computation.3 | async-start | bytes 4325376 | tf_op jit(solution)/shard_map/reduce_scatter | solution.py:46
  249.9 0.7 copy-start.3
  249.9 0.7 copy-start.4
  250.0 1.4 copy-start.2
  250.0 77.6 %copy-start = (bf16[1,32,1,1024]{3,1,2,0:T(8,128)(2,1)S(1)}, bf16[1,32,1,1024]{3,1,2,0:T(8,128)(2,1)}, u32[]{:S(2)}) copy-start(bf16[1,32,1,1024]{3,1,2,0:T(8,128)(2,1)} %param.11) | copy-start | bytes 196612
  250.0 77.6 %copy-start.1 = (s32[1024]{0:T(1024)S(1)}, s32[1024]{0:T(1024)}, u32[]{:S(2)}) copy-start(s32[1024]{0:T(1024)} %param.15) | copy-start | bytes 12292
Sparse Core Ops, SparseCore 0:
  17.6 71.0 all-gather.1
  250.1 77.4 reduce-scatter.1
where the time goes:
time: 339 us; the launch traced here: 338 us
  waiting for transfers between devices  147 us (43%)
  blocking collectives  103 us (30%)
  local copies, waits for them, and re-layouts  47.9 us (14%)
  between operations  14.1 us (4%)
  other arithmetic  12.8 us (4%)
  matrix products  12.7 us (4%)
    all_to_all x1, blocking collectives, body(): lax.all_to_all(pair_block, 'virt', split_axis=3, concat_axis=2, tiled=True)  103 us
    reduce_scatter x1, waiting for transfers between devices, body(): lax.psum_scatter(partial_value, 'virt', scatter_dimension=1, tiled=True)  75.5 us
    all_gather x1, waiting for transfers between devices, body(): pair_block = lax.all_gather(masked, 'occ', axis=1, tiled=True)  71.1 us
    all_to_all x2, local copies, waits for them, and re-layouts, body(): lax.all_to_all(pair_block, 'virt', split_axis=3, concat_axis=2, tiled=True)  19 us
    another operation x1, local copies, waits for them, and re-layouts  13.4 us
    all_gather x1, local copies, waits for them, and re-layouts, body(): pair_block = lax.all_gather(masked, 'occ', axis=1, tiled=True)  12.9 us
    dot_general x1, matrix products, body(): jnp.einsum('skac,ckjb->sajb', relaid, cycle_block, preferred_element_type...  12.7 us
  transfers between devices with their start and end apart: 2, of which 2 were waited for; matrix products, arithmetic and copies ran while one was open for 0% of the time, Pallas kernels for 0%

commit v1 on v0

--- a/solution.py
+++ b/solution.py
@@ -1,7 +1,19 @@
+import functools
+
 import jax
 import jax.numpy as jnp
 from jax import lax
+from jax.experimental import pallas as pl
+from jax.experimental.pallas import tpu as pltpu
 from jax.sharding import PartitionSpec as P
+
+MESH = pl.DeviceIdType.MESH
+CAP = 304
+CAPL = 320
+MCAP = 640
+NSTEP = 6
+BF = jnp.bfloat16
+F32 = jnp.float32
 
 
 def pick_entries(values_table, indices):
@@ -11,24 +23,11 @@
     )
 
 
-def body(
-    amplitudes,
-    cycle_block,
-    drive_term,
-    occ_energy,
-    virt_energy,
-    occ_irrep,
-    virt_irrep,
-    slab_occ,
-    col_occ,
-):
+def general_cycle(amplitudes, cycle_block, occ_irrep, virt_irrep, slab_irrep):
     k_rows = amplitudes.shape[1]
     a_cols = amplitudes.shape[2]
-    j_cols = cycle_block.shape[2]
     occ_pos = lax.axis_index("occ")
     virt_pos = lax.axis_index("virt")
-    slab_irrep = pick_entries(occ_irrep, slab_occ)
-    col_irrep = pick_entries(occ_irrep, col_occ)
     irr_k = lax.dynamic_slice_in_dim(occ_irrep, occ_pos * k_rows, k_rows)
     irr_a = lax.dynamic_slice_in_dim(virt_irrep, virt_pos * a_cols, a_cols)
     parity = (
@@ -44,9 +43,562 @@
         "skac,ckjb->sajb", relaid, cycle_block, preferred_element_type=jnp.float32
     )
     cycle_sum = lax.psum_scatter(partial_value, "virt", scatter_dimension=1, tiled=True)
+    return cycle_sum[0, :, 0, :]
+
+
+def block_transpose(tiles, b1, b0):
+    t = list(tiles)
+    for q in (0, 1):
+        a, b = t[q], t[q + 2]
+        t[q] = jnp.where(b1, pltpu.roll(b, 64, 1), a)
+        t[q + 2] = jnp.where(b1, b, pltpu.roll(a, 64, 1))
+    for q in (0, 2):
+        a, b = t[q], t[q + 1]
+        t[q] = jnp.where(b0, pltpu.roll(b, 32, 1), a)
+        t[q + 1] = jnp.where(b0, b, pltpu.roll(a, 96, 1))
+    return t
+
+
+def kernel(
+    occ_ref, amp, wraw, rank_ref, cls_ref, rankb_ref, amask, wmask, lclass,
+    out,
+    wv, wf, wrep, fold, unfold, foldb, unfoldb, clsb, mbuf, sbuf, sleft, abuf, aleft,
+    xbuf, xleft, zacc, crecv, tsum, t2, r1buf, r2buf, fin,
+    wsem, ysend, yrecv, yloc, ysendl, yrecvl, ylocl,
+    zsend, zrecv, zloc, zsendl, zrecvl, zlocl,
+    xsend, xrecv, fsend, frecv, xsendl, xrecvl, fsendl, frecvl,
+    csend, crecvs, r1send, r1recv, r2send, r2recv,
+):
+    x = lax.axis_index("occ")
+    v = lax.axis_index("virt")
+    y = v // 8
+    z = (v // 2) % 4
+    core = v % 2
+    me8 = z * 2 + core
+
+    def virt_at(yy, zz, cc):
+        return (yy * 4 + zz) * 2 + cc
+
+    right = (x + 1) % 4
+    left = (x + 3) % 4
+
+    def y_peer(o):
+        return (x, virt_at((y + o) % 4, z, core))
+
+    def z_peer(o):
+        oz, oc = o // 2, o % 2
+        return (x, virt_at(y, (z + oz) % 4, (core + oc) % 2))
+
+    def z_slot(o):
+        return ((z + o // 2) % 4) * 2 + (core + o % 2) % 2
+
+    def remote(src, dst, ssem, rsem, dev):
+        return pltpu.make_async_remote_copy(
+            src_ref=src, dst_ref=dst, send_sem=ssem, recv_sem=rsem,
+            device_id=dev, device_id_type=MESH,
+        )
+
+    def y_src(h, k0, nk, yd):
+        return amp.at[pl.ds(k0, nk), pl.ds(16 * h, 16), pl.ds(pl.multiple_of(256 * yd, 256), 256)]
+
+    def y_dst(h, k0, nk):
+        return mbuf.at[h, pl.ds(k0, nk), pl.ds(pl.multiple_of(16 * y, 16), 16), :]
+
+    def y_copy(n, o):
+        h, g = n // 3, n % 3
+        return remote(y_src(h, 8 * g, 8, (y + o) % 4), y_dst(h, 8 * g, 8),
+                      ysend.at[n, o - 1], yrecv.at[n, o - 1], y_peer(o))
+
+    def y_copyl(h, o):
+        return remote(y_src(h, 24, 1, (y + o) % 4), y_dst(h, 24, 1),
+                      ysendl.at[h, o - 1], yrecvl.at[h, o - 1], y_peer(o))
+
+    def y_own(n):
+        h, g = n // 3, n % 3
+        return pltpu.make_async_copy(y_src(h, 8 * g, 8, y), y_dst(h, 8 * g, 8), yloc.at[n])
+
+    def y_ownl(h):
+        return pltpu.make_async_copy(y_src(h, 24, 1, y), y_dst(h, 24, 1), ylocl.at[h])
+
+    def z_dst(n):
+        return abuf.at[n, pl.ds(pl.multiple_of(64 * me8, 64), 64), :]
+
+    def z_dstl(h):
+        return aleft.at[h, pl.ds(pl.multiple_of(16 * me8, 16), 16), :]
+
+    def z_copy(n, o):
+        return remote(sbuf.at[n, z_slot(o)], z_dst(n), zsend.at[n, o - 1], zrecv.at[n, o - 1], z_peer(o))
+
+    def z_copyl(h, o):
+        return remote(sleft.at[h, z_slot(o)], z_dstl(h), zsendl.at[h, o - 1], zrecvl.at[h, o - 1], z_peer(o))
+
+    def z_own(n):
+        return pltpu.make_async_copy(sbuf.at[n, me8], z_dst(n), zloc.at[n])
+
+    def z_ownl(h):
+        return pltpu.make_async_copy(sleft.at[h, me8], z_dstl(h), zlocl.at[h])
+
+    def x_copy(n, side):
+        return remote(xbuf.at[n, 0], xbuf.at[n, 1 + side], xsend.at[n, side], xrecv.at[n, side],
+                      ((right, left)[side], v))
+
+    def f_copy(n, side):
+        lanes = pl.ds(128 * side, 128)
+        return remote(xbuf.at[n, 1 + side, :, lanes], xbuf.at[n, 3, :, lanes],
+                      fsend.at[n, side], frecv.at[n, side], ((right, left)[side], v))
+
+    def x_copyl(h, side):
+        return remote(xleft.at[h, 0], xleft.at[h, 1 + side], xsendl.at[h, side], xrecvl.at[h, side],
+                      ((right, left)[side], v))
+
+    def f_copyl(h, side):
+        return remote(xleft.at[h, 1 + side], xleft.at[h, 3], fsendl.at[h], frecvl.at[h],
+                      ((right, left)[side], v))
+
+    def c_copy(h):
+        return remote(zacc.at[h, :, 1 - core], crecv.at[h], csend.at[h], crecvs.at[h],
+                      (x, virt_at(y, z, 1 - core)))
+
+    def r1_copy(h, axis, o):
+        if axis == 0:
+            yd = (y + o) % 4
+            return remote(tsum.at[h, 0, :, yd], r1buf.at[h, 0, o - 1], r1send.at[h, o - 1],
+                          r1recv.at[h, o - 1], (x, virt_at(yd, z, core)))
+        zd = (z + o) % 4
+        return remote(tsum.at[h, 1, zd], r1buf.at[h, 1, o - 1], r1send.at[h, 2 + o],
+                      r1recv.at[h, 2 + o], (x, virt_at(y, zd, core)))
+
+    def r2_copy(h, axis, o):
+        if axis == 0:
+            zd = (z + o) % 4
+            return remote(t2.at[h, 0, zd], r2buf.at[h, 0, o - 1], r2send.at[h, o - 1],
+                          r2recv.at[h, o - 1], (x, virt_at(y, zd, core)))
+        yd = (y + o) % 4
+        return remote(t2.at[h, 1, yd], r2buf.at[h, 1, o - 1], r2send.at[h, 2 + o],
+                      r2recv.at[h, 2 + o], (x, virt_at(yd, z, core)))
+
+    barrier = pltpu.get_barrier_semaphore()
+    peers = [y_peer(o) for o in (1, 2, 3)] + [z_peer(o) for o in range(1, 8)] + [(right, v), (left, v)]
+    for dev in peers:
+        pl.semaphore_signal(barrier, inc=1, device_id=dev, device_id_type=MESH)
+    pl.semaphore_wait(barrier, len(peers))
+
+    def w_copy(i):
+        rows = pl.ds(800 * i, 800)
+        return pltpu.make_async_copy(wraw.at[rows], wv.at[rows], wsem.at[i])
+
+    for n in range(NSTEP):
+        for o in (2, 1, 3):
+            y_copy(n, o).start()
+        y_own(n).start()
+        if n % 3 == 2:
+            for o in (2, 1, 3):
+                y_copyl(n // 3, o).start()
+            y_ownl(n // 3).start()
+        if n == 1:
+            for i in range(4):
+                w_copy(i).start()
+
+    for h in range(2):
+        row = rank_ref[h]
+        fold[h] = (lax.broadcasted_iota(jnp.int32, (CAPL, 512), 0).astype(F32) == row).astype(F32).astype(BF)
+        col = jnp.transpose(jnp.broadcast_to(row, (128, 512)))
+        for t in range(3):
+            w = min(128, CAPL - 128 * t)
+            lane = lax.broadcasted_iota(jnp.int32, (512, w), 1).astype(F32) + 128.0 * t
+            unfold[h, :, 128 * t:128 * t + w] = (col[:, :w] == lane).astype(F32).astype(BF)
+        clsb[h] = jnp.transpose(jnp.broadcast_to(cls_ref[h], (128, 512)))
+    rowb = rankb_ref[...]
+    unfoldb[...] = (lax.broadcasted_iota(jnp.int32, (MCAP, 1024), 0).astype(F32) == rowb).astype(F32).astype(BF)
+    colb = jnp.transpose(jnp.broadcast_to(rowb, (128, 1024)))
+    for t in range(MCAP // 128):
+        lane = lax.broadcasted_iota(jnp.int32, (1024, 128), 1).astype(F32) + 128.0 * t
+        foldb[:, 128 * t:128 * t + 128] = (colb == lane).astype(F32).astype(BF)
+
+    lane128 = lax.broadcasted_iota(jnp.int32, (1, 128), 1)
+
+    def prepare_w(j, carry):
+        for q in range(4):
+            par = occ_ref[4 * j + q]
+            rows = pl.ds(pl.multiple_of(128 * j + 32 * q, 32), 32)
+            wv[rows, :] = wv[rows, :] * wmask[par]
+        rows = pl.ds(pl.multiple_of(128 * j, 128), 128)
+        wf[rows, :] = jnp.dot(wv[rows, :], foldb[...], preferred_element_type=F32).astype(BF)
+        return carry
+
+    def relay(n):
+        h, g = n // 3, n % 3
+        for o in (1, 2, 3):
+            y_copy(n, o).wait_recv()
+        y_own(n).wait()
+        b1 = (lane128 // 64) % 2 == 1
+        b0 = (lane128 // 32) % 2 == 1
+        for kg in range(2):
+            rowsq = []
+            for q in range(4):
+                k = 8 * g + 4 * kg + q
+                par = occ_ref[25 * x + k]
+                rowsq.append((mbuf[h, k] * amask[h, par]).astype(F32))
+            for t in range(2):
+                res = block_transpose([r[:, 128 * t:128 * t + 128] for r in rowsq], b1, b0)
+                for d in range(4):
+                    sbuf[n, 4 * t + d, :, 128 * kg:128 * kg + 128] = res[d].astype(BF)
+        for o in (4, 5, 2, 3, 6, 7, 1):
+            z_copy(n, o).start()
+        z_own(n).start()
+
+        @pl.when(g == 2)
+        def _():
+            for o in (1, 2, 3):
+                y_copyl(h, o).wait_recv()
+            y_ownl(h).wait()
+            par = occ_ref[25 * x + 24]
+            whole = (mbuf[h, 24] * amask[h, par]).astype(F32)
+            for t in range(2):
+                res = block_transpose(
+                    [whole[16 * q:16 * q + 16, 128 * t:128 * t + 128] for q in range(4)], b1, b0)
+                for d in range(4):
+                    sleft[h, 4 * t + d] = res[d].astype(BF)
+            for o in (4, 5, 2, 3, 6, 7, 1):
+                z_copyl(h, o).start()
+            z_ownl(h).start()
+
+    def fold_step(n):
+        h, g = n // 3, n % 3
+        for o in range(1, 8):
+            z_copy(n, o).wait_recv()
+        z_own(n).wait()
+        xbuf[n, 0] = jnp.dot(fold[h, :CAP], abuf[n], preferred_element_type=F32).astype(BF)
+        for side in range(2):
+            x_copy(n, side).start()
+
+        @pl.when(g == 2)
+        def _():
+            for o in range(1, 8):
+                z_copyl(h, o).wait_recv()
+            z_ownl(h).wait()
+            got = aleft[h].astype(F32)
+            parts = []
+            for s in range(8):
+                for q in range(4):
+                    parts.append(jnp.where(lane128 // 32 == q, got[16 * s:16 * s + 16], 0.0))
+            spread = jnp.concatenate(parts, axis=0).astype(BF)
+            both = jnp.dot(fold[h], spread, preferred_element_type=F32)
+            both = both + pltpu.roll(both, 64, 1)
+            both = both + pltpu.roll(both, 32, 1)
+            packed = both[0:80]
+            for q in range(1, 4):
+                packed = jnp.where(lane128 // 32 == q, both[80 * q:80 * q + 80], packed)
+            xleft[h, 0] = packed.astype(BF)
+            for side in range(2):
+                x_copyl(h, side).start()
+
+    def product(n, slot, first):
+        h, g = n // 3, n % 3
+        src = (x + (0, 3, 1, 2)[slot]) % 4
+        part = jnp.dot(unfold[h, :, :CAP], xbuf[n, slot], preferred_element_type=F32)
+        cls = clsb[h]
+        lane_cls = lclass[4 * src + g]
+        part = jnp.concatenate(
+            [jnp.where(cls == lane_cls[:, 128 * t:128 * t + 128], part[:, 128 * t:128 * t + 128], 0.0)
+             for t in range(2)], axis=1).astype(BF)
+        rows = pl.ds(pl.multiple_of(800 * src + 256 * g, 32), 256)
+        value = jnp.dot(part, wf[rows, :], preferred_element_type=F32)
+        for zz in range(4):
+            for cc in range(2):
+                r0 = (zz * 2 + cc) * 64
+                if first:
+                    zacc[h, zz, cc] = value[r0:r0 + 64]
+                else:
+                    zacc[h, zz, cc] += value[r0:r0 + 64]
+
+    def product_left(h, slot):
+        src = (x + (0, 3, 1, 2)[slot]) % 4
+        got = xleft[h, slot].astype(F32)
+        spread = jnp.concatenate(
+            [jnp.where(lane128 // 32 == q, got, 0.0) for q in range(4)], axis=0).astype(BF)
+        part = jnp.dot(unfold[h], spread, preferred_element_type=F32)
+        lane_cls = lclass[4 * src + 3]
+        part = jnp.where(clsb[h] == lane_cls[:, :128], part, 0.0).astype(BF)
+        one = wf[pl.ds(pl.multiple_of(800 * src + 768, 32), 32), :]
+        value = jnp.dot(part, jnp.concatenate([one] * 4, axis=0), preferred_element_type=F32)
+        for zz in range(4):
+            for cc in range(2):
+                r0 = (zz * 2 + cc) * 64
+                zacc[h, zz, cc] += value[r0:r0 + 64]
+
+    def near_step(n):
+        h, g = n // 3, n % 3
+        for side in range(2):
+            x_copy(n, side).wait_recv()
+            f_copy(n, side).start()
+
+        @pl.when(g == 2)
+        def _():
+            for side in range(2):
+                x_copyl(h, side).wait_recv()
+
+            @pl.when(h == 0)
+            def _():
+                f_copyl(h, 0).start()
+
+            @pl.when(h == 1)
+            def _():
+                f_copyl(h, 1).start()
+
+        @pl.when(g == 0)
+        def _():
+            zacc[h] = jnp.zeros_like(zacc[h])
+
+        for slot in range(3):
+            product(n, slot, False)
+
+        @pl.when(g == 2)
+        def _():
+            for slot in range(3):
+                product_left(h, slot)
+
+    def far_step(n):
+        h, g = n // 3, n % 3
+        for side in range(2):
+            f_copy(n, side).wait_recv()
+        product(n, 3, False)
+
+        @pl.when(g == 2)
+        def _():
+            f_copyl(h, 0).wait_recv()
+            product_left(h, 3)
+            c_copy(h).start()
+
+    def sum_core(h):
+        c_copy(h).wait_recv()
+        for zz in range(4):
+            both = zacc[h, zz, core] + crecv[h, zz]
+            for yy in range(4):
+                for rh in range(2):
+                    r0 = yy * 16 + rh * 8
+                    tsum[h, rh, zz, yy] = both[r0:r0 + 8]
+        for axis in range(2):
+            for o in (2, 1, 3):
+                r1_copy(h, axis, o).start()
+
+    def sum_first(h):
+        for axis in range(2):
+            for o in (1, 2, 3):
+                r1_copy(h, axis, o).wait_recv()
+        for i in range(4):
+            t2[h, 0, i] = tsum[h, 0, i, y] + r1buf[h, 0, 0, i] + r1buf[h, 0, 1, i] + r1buf[h, 0, 2, i]
+            t2[h, 1, i] = tsum[h, 1, z, i] + r1buf[h, 1, 0, i] + r1buf[h, 1, 1, i] + r1buf[h, 1, 2, i]
+        for axis in range(2):
+            for o in (2, 1, 3):
+                r2_copy(h, axis, o).start()
+
+    def sum_second(h):
+        for axis in range(2):
+            for o in (1, 2, 3):
+                r2_copy(h, axis, o).wait_recv()
+        fin[h, 0] = t2[h, 0, z] + r2buf[h, 0, 0] + r2buf[h, 0, 1] + r2buf[h, 0, 2]
+        fin[h, 1] = t2[h, 1, y] + r2buf[h, 1, 0] + r2buf[h, 1, 1] + r2buf[h, 1, 2]
+
+    def step(n, carry):
+        @pl.when(n < NSTEP)
+        def _():
+            relay(n)
+
+        @pl.when(n == 0)
+        def _():
+            for i in range(4):
+                w_copy(i).wait()
+            lax.fori_loop(0, 13, prepare_w, 0)
+
+        @pl.when(jnp.logical_and(n >= 1, n < NSTEP + 1))
+        def _():
+            fold_step(n - 1)
+
+        @pl.when(n == 1)
+        def _():
+            lax.fori_loop(13, 25, prepare_w, 0)
+
+        @pl.when(jnp.logical_and(n >= 2, n < NSTEP + 2))
+        def _():
+            near_step(n - 2)
+
+        @pl.when(jnp.logical_or(n == 6, n == 9))
+        def _():
+            sum_core(n // 3 - 2)
+
+        @pl.when(jnp.logical_or(n == 7, n == 10))
+        def _():
+            sum_first(n // 3 - 2)
+
+        @pl.when(jnp.logical_and(n >= 3, n < NSTEP + 3))
+        def _():
+            far_step(n - 3)
+
+        return carry
+
+    lax.fori_loop(0, 11, step, 0)
+    sum_second(0)
+    sum_second(1)
+
+    total = jnp.concatenate([fin[0, 0], fin[0, 1], fin[1, 0], fin[1, 1]], axis=0)
+    hi = total.astype(BF)
+    rest = total - hi.astype(F32)
+    mid = rest.astype(BF)
+    low = (rest - mid.astype(F32)).astype(BF)
+    table = unfoldb[...]
+    out[...] = (
+        jnp.dot(hi, table, preferred_element_type=F32)
+        + jnp.dot(mid, table, preferred_element_type=F32)
+    ) + jnp.dot(low, table, preferred_element_type=F32)
+
+    def finish(n, carry):
+        for o in (1, 2, 3):
+            y_copy(n, o).wait_send()
+        for o in range(1, 8):
+            z_copy(n, o).wait_send()
+        for side in range(2):
+            x_copy(n, side).wait_send()
+            f_copy(n, side).wait_send()
+        return carry
+
+    lax.fori_loop(0, NSTEP, finish, 0)
+
+    def finish_half(h, carry):
+        for o in (1, 2, 3):
+            y_copyl(h, o).wait_send()
+        for o in range(1, 8):
+            z_copyl(h, o).wait_send()
+        for side in range(2):
+            x_copyl(h, side).wait_send()
+        f_copyl(h, 0).wait_send()
+        c_copy(h).wait_send()
+        for axis in range(2):
+            for o in (1, 2, 3):
+                r1_copy(h, axis, o).wait_send()
+                r2_copy(h, axis, o).wait_send()
+        return carry
+
+    lax.fori_loop(0, 2, finish_half, 0)
+
+
+def folded_cycle(amplitudes, cycle_block, occ_irrep, virt_irrep, slab_irrep, col_irrep_here, rank_half, rank_all):
+    x = lax.axis_index("occ")
+    v = lax.axis_index("virt")
+    y, z, core = v // 8, (v // 2) % 4, v % 2
+    slab = slab_irrep[0]
+    amp = amplitudes.reshape(25, 32, 1024)
+    wraw = jnp.transpose(cycle_block, (1, 2, 0, 3)).reshape(3200, 1024)
+    vi = virt_irrep.reshape(4, 4, 2, 2, 16)
+    half_cls = jnp.transpose(vi, (3, 1, 2, 0, 4)).reshape(2, 1, 512).astype(F32)
+    mine = lax.dynamic_slice(vi, (0, z, core, 0, 0), (4, 1, 1, 2, 16)).reshape(4, 2, 16)
+    row_par = jnp.transpose(mine, (1, 0, 2)).reshape(2, 64)
+    c_mid = lax.dynamic_slice_in_dim(virt_irrep, 256 * y, 256)
+    two = jnp.arange(2, dtype=jnp.int32)
+    amask = (
+        (slab + two[None, :, None, None] + row_par[:, None, :, None] + c_mid[None, None, None, :]) % 2 == 0
+    ).astype(BF)
+    c_here = lax.dynamic_slice_in_dim(virt_irrep, 32 * v, 32)
+    wmask = (
+        (two[:, None, None] + c_here[None, :, None] + virt_irrep[None, None, :] + col_irrep_here) % 2 == 0
+    ).astype(BF)
+    kk = occ_irrep.reshape(4, 25)
+    main = (kk[:, :24, None] + c_here[None, None, :] + slab).reshape(4, 3, 256)
+    last = jnp.broadcast_to(kk[:, 24:, None, None] + c_here[None, None, None, :] + slab, (4, 1, 8, 32)).reshape(4, 1, 256)
+    lclass = (jnp.concatenate([main, last], axis=1) % 2).reshape(16, 1, 256).astype(F32)
+
+    dma = pltpu.SemaphoreType.DMA
+    vmem = pl.BlockSpec(memory_space=pltpu.VMEM)
+    hbm = pl.BlockSpec(memory_space=pl.ANY)
+    scratch = [
+        pltpu.VMEM((3200, 1024), BF),
+        pltpu.VMEM((3200, MCAP), BF),
+        pltpu.VMEM((8, 128), BF),
+        pltpu.VMEM((2, CAPL, 512), BF),
+        pltpu.VMEM((2, 512, CAPL), BF),
+        pltpu.VMEM((1024, MCAP), BF),
+        pltpu.VMEM((MCAP, 1024), BF),
+        pltpu.VMEM((2, 512, 128), F32),
+        pltpu.VMEM((2, 25, 64, 256), BF),
+        pltpu.VMEM((NSTEP, 8, 64, 256), BF),
+        pltpu.VMEM((2, 8, 16, 128), BF),
+        pltpu.VMEM((NSTEP, 512, 256), BF),
+        pltpu.VMEM((2, 128, 128), BF),
+        pltpu.VMEM((NSTEP, 4, CAP, 256), BF),
+        pltpu.VMEM((2, 4, 80, 128), BF),
+        pltpu.VMEM((2, 4, 2, 64, MCAP), F32),
+        pltpu.VMEM((2, 4, 64, MCAP), F32),
+        pltpu.VMEM((2, 2, 4, 4, 8, MCAP), F32),
+        pltpu.VMEM((2, 2, 4, 8, MCAP), F32),
+        pltpu.VMEM((2, 2, 3, 4, 8, MCAP), F32),
+        pltpu.VMEM((2, 2, 3, 8, MCAP), F32),
+        pltpu.VMEM((2, 2, 8, MCAP), F32),
+        dma((4,)),
+        dma((NSTEP, 3)), dma((NSTEP, 3)), dma((NSTEP,)),
+        dma((2, 3)), dma((2, 3)), dma((2,)),
+        dma((NSTEP, 7)), dma((NSTEP, 7)), dma((NSTEP,)),
+        dma((2, 7)), dma((2, 7)), dma((2,)),
+        dma((NSTEP, 2)), dma((NSTEP, 2)), dma((NSTEP, 2)), dma((NSTEP, 2)),
+        dma((2, 2)), dma((2, 2)), dma((2,)), dma((2,)),
+        dma((2,)), dma((2,)),
+        dma((2, 6)), dma((2, 6)), dma((2, 6)), dma((2, 6)),
+    ]
+    return pl.pallas_call(
+        kernel,
+        out_shape=jax.ShapeDtypeStruct((32, 1024), F32),
+        in_specs=[pl.BlockSpec(memory_space=pltpu.SMEM), hbm, hbm] + [vmem] * 6,
+        out_specs=vmem,
+        scratch_shapes=scratch,
+        compiler_params=pltpu.CompilerParams(
+            collective_id=0, has_side_effects=True, vmem_limit_bytes=52 * 2**20
+        ),
+        name="cycle",
+    )(occ_irrep, amp, wraw, rank_half, half_cls, rank_all, amask, wmask, lclass)
+
+
+def ranks(cls):
+    n = cls.shape[-1]
+    same = cls[..., :, None] == cls[..., None, :]
+    before = jnp.arange(n)[:, None] < jnp.arange(n)[None, :]
+    return jnp.sum(jnp.where(same & before, 1, 0), axis=-2, dtype=jnp.int32)
+
+
+def body(
+    amplitudes,
+    cycle_block,
+    drive_term,
+    occ_energy,
+    virt_energy,
+    occ_irrep,
+    virt_irrep,
+    slab_occ,
+    col_occ,
+):
+    a_cols = amplitudes.shape[2]
+    j_cols = cycle_block.shape[2]
+    occ_pos = lax.axis_index("occ")
+    virt_pos = lax.axis_index("virt")
+    slab_irrep = pick_entries(occ_irrep, slab_occ)
+    col_irrep = pick_entries(occ_irrep, col_occ)
+    irr_a = lax.dynamic_slice_in_dim(virt_irrep, virt_pos * a_cols, a_cols)
+    irr_cols = lax.dynamic_slice_in_dim(col_irrep, occ_pos * j_cols, j_cols)
+
+    half = jnp.transpose(virt_irrep.reshape(4, 4, 2, 2, 16), (3, 1, 2, 0, 4)).reshape(2, 512)
+    rank_half = ranks(half)
+    rank_all = ranks(virt_irrep)
+    fits = jnp.logical_and(jnp.max(rank_half) < CAP, jnp.max(rank_all) < MCAP)
+
+    cycle_sum = lax.cond(
+        fits,
+        lambda *args: folded_cycle(*args),
+        lambda amp, w, occ, virt, slab, *rest: general_cycle(amp, w, occ, virt, slab),
+        amplitudes, cycle_block, occ_irrep, virt_irrep, slab_irrep, irr_cols[0],
+        rank_half.reshape(2, 1, 512).astype(F32), rank_all.reshape(1, 1024).astype(F32),
+    )
+    cycle_sum = cycle_sum.reshape(1, a_cols, j_cols, 1024)
+
     e_slab = pick_entries(occ_energy, slab_occ)
     e_cols = lax.dynamic_slice_in_dim(pick_entries(occ_energy, col_occ), occ_pos * j_cols, j_cols)
-    irr_cols = lax.dynamic_slice_in_dim(col_irrep, occ_pos * j_cols, j_cols)
     e_rows = lax.dynamic_slice_in_dim(virt_energy, virt_pos * a_cols, a_cols)
     divisor = (
         e_rows[None, :, None, None]

time: 339 us -> 111 us (0.33)
  waiting for transfers between devices: 147 us -> 0 us
  blocking collectives: 103 us -> 0 us
  Pallas kernels: 0 us -> 74 us
  local copies, waits for them, and re-layouts: 47.9 us -> 6.21 us
  matrix products: 12.7 us -> 0 us
    all_to_all x1 -> x0, blocking collectives: 103 us -> none  [body(): lax.all_to_all(pair_block, 'virt', split_axis=3, concat_axis=2, tiled=True)]
    reduce_scatter x1 -> x0, waiting for transfers between devices: 75.5 us -> none  [body(): lax.psum_scatter(partial_value, 'virt', scatter_dimension=1, tiled=True)]
    pallas_call x0 -> x1, Pallas kernels: none -> 74 us  [folded_cycle(): pl.pallas_call(kernel, out_shape=jax.ShapeDtypeStruct((32, 1024), F32), i...]
    all_gather x1 -> x0, waiting for transfers between devices: 71.1 us -> none  [body(): pair_block = lax.all_gather(masked, 'occ', axis=1, tiled=True)]
    all_to_all x2 -> x0, local copies, waits for them, and re-layouts: 19 us -> none  [body(): lax.all_to_all(pair_block, 'virt', split_axis=3, concat_axis=2, tiled=True)]
    another operation x1 -> x0, local copies, waits for them, and re-layouts: 13.4 us -> none
    all_gather x1 -> x0, local copies, waits for them, and re-layouts: 12.9 us -> none  [body(): pair_block = lax.all_gather(masked, 'occ', axis=1, tiled=True)]
    dot_general x1 -> x0, matrix products: 12.7 us -> none  [body(): jnp.einsum('skac,ckjb->sajb', relaid, cycle_block, preferred_element_type...]
  transfers between devices with their start and end apart: 2 -> 0, of which waited for: 2 -> 0; matrix products, arithmetic and copies ran while one was open for 0% -> 0% of each run, Pallas kernels for 0% -> 0%
where the time goes in v1:
time: 111 us
  Pallas kernels  74 us (67%)
  between operations  15.4 us (14%)
  other arithmetic  14.9 us (13%)
  local copies, waits for them, and re-layouts  6.21 us (6%)
    pallas_call x1, Pallas kernels, folded_cycle(): pl.pallas_call(kernel, out_shape=jax.ShapeDtypeStruct((32, 1024), F32), i...  74 us
    reduce_sum x4, other arithmetic, pick_entries(): jnp.sum(jnp.where(hits, values_table[None, :], jnp.zeros((), values_table...  3 us
    select_n x1, other arithmetic, body(): return jnp.where(out_parity % 2 == 0, value, jnp.zeros((), jnp.float32))  2.65 us

profile of v1, /device:TPU:1, one launch (start us, length us, event | category | flops | bytes accessed | tf_op | source)
XLA Modules:
  0.0 110.8 jit_solution(12191956638169552490)
XLA Ops:
  6.5 0.8 reshape.477
  7.3 0.1 eq.112
  7.4 0.1 iota_compare_fusion.1
  7.5 0.5 select_reduce_fusion.1
  8.0 0.6 reduce_max.18
  9.3 1.3 %select_reduce_fusion = s32[1024]{0:T(1024)S(1)} fusion(s32[1024]{0:T(1024)} %param.17), kind=kLoop, calls=%fused_computation.43 | loop fusion | flops 5241856 | bytes 8192 | tf_op jit(solution)/shard_map/reduce_sum | solution.py:563
  10.6 0.6 reduce_max.19
  12.6 1.4 %fusion.24 = s32[]{:T(128)} fusion(s32[100]{0:T(128)} %param.16, s32[]{:T(128)} %bitcast.37), kind=kLoop, calls=%fused_computation.61 | loop fusion | flops 299 | bytes 408 | tf_op jit(solution)/shard_map/reduce_sum | solution.py:21
  14.0 0.9 select_reduce_fusion.3
  14.8 0.6 dynamic_slice.28
  15.4 0.0 copy-start.3
  15.4 0.0 copy-start.4
  15.4 0.0 copy-start.2
  15.4 0.0 copy-start
  15.4 0.0 copy-start.1
  15.5 82.3 %conditional.1 = (f32[1,32,1,1024]{3,2,1,0:T(1,128)S(1)}) conditional(s32[]{:T(128)} %convert_element_type.41, (s32[1]{0:T(128)}, s32[100]{0:T(128)}, s32[1024]{0:T(1024)}, bf16[1,25,32,1024]{3,2,1,0:T(8,128)(2,1)}, bf16[32,100,1,1024]{3,0,2,1:T(8,128)(2,1)}) %tuple.13, (bf16[1,25,32,1024]{3,2,1,0:T(8,128)(2,1)}, ...), branch_computations={%region_6.8_spmd, %region_8.9_spmd} | conditional | flops 6722356224 | bytes 130493648 | solution.py:591
  15.7 0.8 reshape.472
  16.6 0.1 convert_element_type.32.cls_ref
  16.7 0.8 dynamic_slice.21
  17.4 0.1 add.297
  17.5 0.7 iota_add_fusion.1
  18.2 0.1 broadcast_add_fusion.1
  18.3 0.2 fusion.17.amask
  18.5 0.8 dynamic_slice.22
  19.3 1.5 %fusion.16.wmask = bf16[2,32,1024]{2,1,0:T(8,128)(2,1)S(1)} fusion(s32[]{:T(128)} %get-tuple-element.51, s32[1024]{0:T(1024)} %get-tuple-element.48, s32[2,32]{1,0:T(2,128)S(1)} %iota_add_fusion), kind=kLoop, calls=%fused_computation.27 | loop fusion | flops 983040 | bytes 135428 | tf_op jit(solution)/shard_map/cond/branch_1_fun/convert_element_type | solution.py:504
  20.8 0.7 reshape.474
  21.5 0.2 slice_reduce_fusion
  21.7 0.8 add_add_fusion.1
  22.5 0.1 broadcast_in_dim.46
  22.6 0.1 add.315
  22.6 0.1 add.316
  22.7 0.1 add.318
  22.8 0.7 add_add_fusion
  23.6 0.1 fusion.18.lclass
  23.6 74.0 %cycle.1 = f32[32,1024]{1,0:T(8,128)S(1)} custom-call(s32[100]{0:T(128)} %get-tuple-element.44.occ_ref, bf16[25,32,1024]{2,1,0:T(8,128)(2,1)} %bitcast.46, bf16[3200,1024]{1,0:T(8,128)(2,1)} %bitcast.45, f32[2,1,512]{2,1,0:T(1,128)S(1)} %convert_element_type.29.rank_ref, f32[2,1,512]{2,1,0:T(1,128)S(1)} %convert_element_type.32.cls_ref, ...), custom_call_target="tpu_custom_call" | custom-call | tf_op jit(solution)/shard_map/cond/branch_1_fun/cycle/pallas_call | solution.py:546
  97.6 0.1 copy.61
  97.7 0.0 copy-done.3
  97.7 0.0 copy-done.4
  97.8 0.2 select_reduce_fusion.2
  97.9 0.7 dynamic_slice.30
  98.6 0.6 fusion.25
  99.2 0.0 copy-done.2
  99.2 0.1 dynamic_slice.29
  99.3 2.1 %add_add_fusion.2 = s32[32]{0:T(128)S(1)} fusion(s32[1024]{0:T(1024)} %param.17, s32[]{:T(128)S(6)} %select_n.133, s32[]{:T(128)} %bitcast.19, s32[]{:T(128)} %fusion.24), kind=kLoop, calls=%fused_computation.63 | loop fusion | flops 64 | bytes 268 | tf_op jit(solution)/shard_map/add | solution.py:610
  101.3 0.0 copy-done
  101.3 0.0 copy-done.1
  101.3 2.6 %compare_select_fusion.4 = f32[1,32,1,1024]{3,2,1,0:T(1,128)} fusion(f32[1,32,1,1024]{3,2,1,0:T(1,128)S(1)} %get-tuple-element.117, bf16[1,32,1,1024]{3,1,2,0:T(8,128)(2,1)S(1)} %copy-done.1, f32[]{:T(128)} %bitcast.22, f32[]{:T(128)} %fusion.25, f32[1024]{0:T(1024)S(1)} %copy-done.2, s32[1024]{0:T(1024)S(1)} %copy-done, f32[32]{0:T(128)S(1)} %dynamic_slice.29, ...), kind=kLoop, calls=%fused_computation.50 | loop fusion | flops 655360 | bytes 336136 | tf_op jit(solution)/shard_map/jit(_where)/select_n | solution.py:616
  (13 shorter events, 0.1 us)
Async XLA Ops:
  15.4 82.3 %copy-start.3 = (s32[4]{0:T(128)S(1)}, s32[4]{0:T(128)}, u32[]{:S(2)}) copy-start(s32[4]{0:T(128)} %param.19) | copy-start | bytes 52
  15.4 82.3 %copy-start.4 = (f32[100]{0:T(128)S(1)}, f32[100]{0:T(128)}, u32[]{:S(2)}) copy-start(f32[100]{0:T(128)} %param.14) | copy-start | bytes 1204
  15.4 83.8 %copy-start.2 = (f32[1024]{0:T(1024)S(1)}, f32[1024]{0:T(1024)}, u32[]{:S(2)}) copy-start(f32[1024]{0:T(1024)} %param.15) | copy-start | bytes 12292
  15.4 85.9 %copy-start = (s32[1024]{0:T(1024)S(1)}, s32[1024]{0:T(1024)}, u32[]{:S(2)}) copy-start(s32[1024]{0:T(1024)} %param.17) | copy-start | bytes 12292
  15.4 85.9 %copy-start.1 = (bf16[1,32,1,1024]{3,1,2,0:T(8,128)(2,1)S(1)}, bf16[1,32,1,1024]{3,1,2,0:T(8,128)(2,1)}, u32[]{:S(2)}) copy-start(bf16[1,32,1,1024]{3,1,2,0:T(8,128)(2,1)} %param.13) | copy-start | bytes 196612

commit v2 on v1

--- a/solution.py
+++ b/solution.py
@@ -1,5 +1,3 @@
-import functools
-
 import jax
 import jax.numpy as jnp
 from jax import lax
@@ -12,6 +10,7 @@
 CAPL = 320
 MCAP = 640
 NSTEP = 6
+OUT = (1, 32, 1, 1024)
 BF = jnp.bfloat16
 F32 = jnp.float32
 
@@ -23,27 +22,33 @@
     )
 
 
-def general_cycle(amplitudes, cycle_block, occ_irrep, virt_irrep, slab_irrep):
-    k_rows = amplitudes.shape[1]
-    a_cols = amplitudes.shape[2]
-    occ_pos = lax.axis_index("occ")
-    virt_pos = lax.axis_index("virt")
-    irr_k = lax.dynamic_slice_in_dim(occ_irrep, occ_pos * k_rows, k_rows)
-    irr_a = lax.dynamic_slice_in_dim(virt_irrep, virt_pos * a_cols, a_cols)
-    parity = (
-        slab_irrep[:, None, None, None]
-        + irr_k[None, :, None, None]
-        + irr_a[None, None, :, None]
-        + virt_irrep[None, None, None, :]
-    )
-    masked = jnp.where(parity % 2 == 0, amplitudes, jnp.zeros((), amplitudes.dtype))
-    pair_block = lax.all_gather(masked, "occ", axis=1, tiled=True)
-    relaid = lax.all_to_all(pair_block, "virt", split_axis=3, concat_axis=2, tiled=True)
-    partial_value = jnp.einsum(
-        "skac,ckjb->sajb", relaid, cycle_block, preferred_element_type=jnp.float32
-    )
-    cycle_sum = lax.psum_scatter(partial_value, "virt", scatter_dimension=1, tiled=True)
-    return cycle_sum[0, :, 0, :]
+def spread_all(block, axis, count):
+    return lax.all_to_all(jnp.broadcast_to(block[None], (count,) + block.shape), axis, 0, 0, tiled=True)
+
+
+def general_update(amp, wraw, drive, occ_irrep, virt_irrep, slab_occ, col_occ, occ_energy, virt_energy):
+    x = lax.axis_index("occ")
+    v = lax.axis_index("virt")
+    slab_irrep = pick_entries(occ_irrep, slab_occ)[0]
+    col_here = lax.dynamic_slice_in_dim(col_occ, x, 1)
+    col_irrep = pick_entries(occ_irrep, col_here)[0]
+    irr_k = lax.dynamic_slice_in_dim(occ_irrep, x * 25, 25)
+    irr_a = lax.dynamic_slice_in_dim(virt_irrep, v * 32, 32)
+    parity = slab_irrep + irr_k[:, None, None] + irr_a[None, :, None] + virt_irrep[None, None, :]
+    masked = jnp.where(parity % 2 == 0, amp, jnp.zeros((), amp.dtype))
+    pair_block = spread_all(masked, "occ", 4).reshape(100, 32, 1024)
+    relaid = lax.all_to_all(pair_block, "virt", split_axis=2, concat_axis=1, tiled=True)
+    w = wraw.reshape(100, 32, 1024)
+    partial_value = jnp.einsum("kac,kcb->ab", relaid, w, preferred_element_type=F32)
+    parts = lax.all_to_all(partial_value.reshape(32, 32, 1024), "virt", 0, 0, tiled=True)
+    cycle_sum = jnp.sum(parts, axis=0)
+    e_slab = pick_entries(occ_energy, slab_occ)[0]
+    e_col = pick_entries(occ_energy, col_here)[0]
+    e_rows = lax.dynamic_slice_in_dim(virt_energy, v * 32, 32)
+    divisor = e_rows[:, None] + virt_energy[None, :] - e_slab - e_col
+    out_parity = slab_irrep + irr_a[:, None] + col_irrep + virt_irrep[None, :]
+    value = (drive.astype(F32) + cycle_sum) / divisor
+    return jnp.where(out_parity % 2 == 0, value, jnp.zeros((), F32)).reshape(OUT)
 
 
 def block_transpose(tiles, b1, b0):
@@ -60,10 +65,10 @@
 
 
 def kernel(
-    occ_ref, amp, wraw, rank_ref, cls_ref, rankb_ref, amask, wmask, lclass,
+    occ_ref, slab_ref, colo_ref, eocc_ref, virt_ref, evirt_ref, drive_ref, amp, wraw,
     out,
-    wv, wf, wrep, fold, unfold, foldb, unfoldb, clsb, mbuf, sbuf, sleft, abuf, aleft,
-    xbuf, xleft, zacc, crecv, tsum, t2, r1buf, r2buf, fin,
+    wv, wf, amask, wmask, vrow, col, crow, rankb, rankh, fold, unfold, foldb, unfoldb, clsb, mbuf, sbuf, sleft, abuf, aleft,
+    xbuf, xleft, zacc, crecv, tsum, t2, r1buf, r2buf, fin, ecol,
     wsem, ysend, yrecv, yloc, ysendl, yrecvl, ylocl,
     zsend, zrecv, zloc, zsendl, zrecvl, zlocl,
     xsend, xrecv, fsend, frecv, xsendl, xrecvl, fsendl, frecvl,
@@ -199,23 +204,83 @@
             for i in range(4):
                 w_copy(i).start()
 
+    lane128 = lax.broadcasted_iota(jnp.int32, (1, 128), 1)
+
+    slab = slab_ref[0]
+    slab_irr = occ_ref[slab]
+    colo = colo_ref[x]
+    col_irr = occ_ref[colo]
+
+    def flip(row, par):
+        return jnp.where(par % 2 == 1, 1.0 - row, row)
+
+    def one_hot(cond):
+        return cond.astype(F32).astype(BF)
+
+    vrow[...] = virt_ref[...].astype(F32)
+    col[...] = jnp.transpose(jnp.broadcast_to(vrow[...], (128, 1024)))
     for h in range(2):
-        row = rank_ref[h]
-        fold[h] = (lax.broadcasted_iota(jnp.int32, (CAPL, 512), 0).astype(F32) == row).astype(F32).astype(BF)
-        col = jnp.transpose(jnp.broadcast_to(row, (128, 512)))
-        for t in range(3):
-            w = min(128, CAPL - 128 * t)
-            lane = lax.broadcasted_iota(jnp.int32, (512, w), 1).astype(F32) + 128.0 * t
-            unfold[h, :, 128 * t:128 * t + w] = (col[:, :w] == lane).astype(F32).astype(BF)
-        clsb[h] = jnp.transpose(jnp.broadcast_to(cls_ref[h], (128, 512)))
-    rowb = rankb_ref[...]
-    unfoldb[...] = (lax.broadcasted_iota(jnp.int32, (MCAP, 1024), 0).astype(F32) == rowb).astype(F32).astype(BF)
-    colb = jnp.transpose(jnp.broadcast_to(rowb, (128, 1024)))
-    for t in range(MCAP // 128):
-        lane = lax.broadcasted_iota(jnp.int32, (1024, 128), 1).astype(F32) + 128.0 * t
-        foldb[:, 128 * t:128 * t + 128] = (colb == lane).astype(F32).astype(BF)
-
-    lane128 = lax.broadcasted_iota(jnp.int32, (1, 128), 1)
+        rows = jnp.concatenate(
+            [col[pl.ds(pl.multiple_of(256 * yy + 32 * (me8) + 16 * h, 16), 16), :] for yy in range(4)], axis=0)
+        for t in range(2):
+            c_mid = vrow[:, pl.ds(pl.multiple_of(256 * y + 128 * t, 128), 128)]
+            for par in range(2):
+                amask[h, par, :, 128 * t:128 * t + 128] = one_hot(rows == flip(c_mid, slab_irr + par))
+
+    def rank_tables():
+        def chunk(i, carry):
+            rows = lax.broadcasted_iota(jnp.int32, (128, 1024), 0) + 128 * i
+            cols = lax.broadcasted_iota(jnp.int32, (128, 1024), 1)
+            before = cols < rows
+            ones = col[...].astype(BF)
+            count = jnp.dot(one_hot(before), ones, preferred_element_type=F32)
+            same = ((rows ^ cols) & 16) == 0
+            count_h = jnp.dot(one_hot(before & same), ones, preferred_element_type=F32)
+            here = pl.ds(pl.multiple_of(128 * i, 128), 128)
+            cls = col[here, :]
+            rows = lax.broadcasted_iota(jnp.int32, (128, 128), 0) + 128 * i
+            rankb[here, :] = jnp.where(cls == 1.0, count, rows.astype(F32) - count)
+            rows_h = (rows >> 5) * 16 + (rows & 15)
+            count_h = jnp.where(cls == 1.0, count_h, rows_h.astype(F32) - count_h)
+            for b in range(8):
+                place = (((i % 2) * 4 + b // 2) * 4 + i // 2) * 16
+                rankh[b % 2, pl.ds(pl.multiple_of(place, 16), 16), :] = count_h[16 * b:16 * b + 16]
+                clsb[b % 2, pl.ds(pl.multiple_of(place, 16), 16), :] = cls[16 * b:16 * b + 16]
+            return carry
+
+        lax.fori_loop(0, 8, chunk, 0)
+        for h in range(2):
+            row = jnp.transpose(rankh[h])[0:1]
+            fold[h] = one_hot(lax.broadcasted_iota(jnp.int32, (CAPL, 512), 0).astype(F32) == row)
+
+    def more_tables():
+        for h in range(2):
+            for t in range(3):
+                w = min(128, CAPL - 128 * t)
+                lane = lax.broadcasted_iota(jnp.int32, (512, w), 1).astype(F32) + 128.0 * t
+                unfold[h, :, 128 * t:128 * t + w] = one_hot(rankh[h][:, :w] == lane)
+        for t in range(MCAP // 128):
+            lane = lax.broadcasted_iota(jnp.int32, (1024, 128), 1).astype(F32) + 128.0 * t
+            foldb[:, 128 * t:128 * t + 128] = one_hot(rankb[...] == lane)
+        crows = col[pl.ds(pl.multiple_of(32 * v, 32), 32), :]
+        for par in range(2):
+            for t in range(8):
+                row = flip(vrow[:, 128 * t:128 * t + 128], col_irr + par)
+                wmask[par, :, 128 * t:128 * t + 128] = one_hot(crows == row)
+        sub = lax.broadcasted_iota(jnp.int32, (32, 128), 0)
+        hit = sub == lax.broadcasted_iota(jnp.int32, (32, 128), 1) % 32
+        crow[...] = jnp.sum(jnp.where(hit, crows, 0.0), axis=0, keepdims=True)
+
+    def last_tables():
+        row = jnp.transpose(rankb[...])[0:1]
+        unfoldb[...] = one_hot(lax.broadcasted_iota(jnp.int32, (MCAP, 1024), 0).astype(F32) == row)
+
+    def lane_class(src, k0, step):
+        row = flip(crow[...], slab_irr + occ_ref[25 * src + k0])
+        for q in range(1, 4):
+            other = flip(crow[...], slab_irr + occ_ref[25 * src + k0 + q * step])
+            row = jnp.where(lane128 // 32 == q, other, row)
+        return row
 
     def prepare_w(j, carry):
         for q in range(4):
@@ -293,24 +358,20 @@
             for side in range(2):
                 x_copyl(h, side).start()
 
-    def product(n, slot, first):
+    def product(n, slot):
         h, g = n // 3, n % 3
         src = (x + (0, 3, 1, 2)[slot]) % 4
         part = jnp.dot(unfold[h, :, :CAP], xbuf[n, slot], preferred_element_type=F32)
         cls = clsb[h]
-        lane_cls = lclass[4 * src + g]
         part = jnp.concatenate(
-            [jnp.where(cls == lane_cls[:, 128 * t:128 * t + 128], part[:, 128 * t:128 * t + 128], 0.0)
+            [jnp.where(cls == lane_class(src, 8 * g + 4 * t, 1), part[:, 128 * t:128 * t + 128], 0.0)
              for t in range(2)], axis=1).astype(BF)
         rows = pl.ds(pl.multiple_of(800 * src + 256 * g, 32), 256)
         value = jnp.dot(part, wf[rows, :], preferred_element_type=F32)
         for zz in range(4):
             for cc in range(2):
                 r0 = (zz * 2 + cc) * 64
-                if first:
-                    zacc[h, zz, cc] = value[r0:r0 + 64]
-                else:
-                    zacc[h, zz, cc] += value[r0:r0 + 64]
+                zacc[h, zz, cc] += value[r0:r0 + 64]
 
     def product_left(h, slot):
         src = (x + (0, 3, 1, 2)[slot]) % 4
@@ -318,8 +379,7 @@
         spread = jnp.concatenate(
             [jnp.where(lane128 // 32 == q, got, 0.0) for q in range(4)], axis=0).astype(BF)
         part = jnp.dot(unfold[h], spread, preferred_element_type=F32)
-        lane_cls = lclass[4 * src + 3]
-        part = jnp.where(clsb[h] == lane_cls[:, :128], part, 0.0).astype(BF)
+        part = jnp.where(clsb[h] == lane_class(src, 24, 0), part, 0.0).astype(BF)
         one = wf[pl.ds(pl.multiple_of(800 * src + 768, 32), 32), :]
         value = jnp.dot(part, jnp.concatenate([one] * 4, axis=0), preferred_element_type=F32)
         for zz in range(4):
@@ -351,7 +411,7 @@
             zacc[h] = jnp.zeros_like(zacc[h])
 
         for slot in range(3):
-            product(n, slot, False)
+            product(n, slot)
 
         @pl.when(g == 2)
         def _():
@@ -362,7 +422,7 @@
         h, g = n // 3, n % 3
         for side in range(2):
             f_copy(n, side).wait_recv()
-        product(n, 3, False)
+        product(n, 3)
 
         @pl.when(g == 2)
         def _():
@@ -407,17 +467,26 @@
 
         @pl.when(n == 0)
         def _():
+            rank_tables()
+
+        @pl.when(jnp.logical_and(n >= 1, n < NSTEP + 1))
+        def _():
+            fold_step(n - 1)
+
+        @pl.when(n == 1)
+        def _():
+            more_tables()
             for i in range(4):
                 w_copy(i).wait()
-            lax.fori_loop(0, 13, prepare_w, 0)
-
-        @pl.when(jnp.logical_and(n >= 1, n < NSTEP + 1))
-        def _():
-            fold_step(n - 1)
-
-        @pl.when(n == 1)
-        def _():
-            lax.fori_loop(13, 25, prepare_w, 0)
+            lax.fori_loop(0, 9, prepare_w, 0)
+
+        @pl.when(n == 2)
+        def _():
+            lax.fori_loop(9, 25, prepare_w, 0)
+
+        @pl.when(n == 3)
+        def _():
+            last_tables()
 
         @pl.when(jnp.logical_and(n >= 2, n < NSTEP + 2))
         def _():
@@ -446,11 +515,23 @@
     rest = total - hi.astype(F32)
     mid = rest.astype(BF)
     low = (rest - mid.astype(F32)).astype(BF)
-    table = unfoldb[...]
-    out[...] = (
-        jnp.dot(hi, table, preferred_element_type=F32)
-        + jnp.dot(mid, table, preferred_element_type=F32)
-    ) + jnp.dot(low, table, preferred_element_type=F32)
+    tile = evirt_ref[:, pl.ds(pl.multiple_of(128 * (v // 4), 128), 128)]
+    e_rows = jnp.transpose(jnp.broadcast_to(tile, (128, 128)))
+    ecol[...] = e_rows
+    e_here = ecol[pl.ds(pl.multiple_of(32 * (v % 4), 32), 32), :]
+    e_slab = eocc_ref[slab]
+    e_col = eocc_ref[colo]
+    cls = col[pl.ds(pl.multiple_of(32 * v, 32), 32), :]
+    for t in range(8):
+        lanes = slice(128 * t, 128 * t + 128)
+        table = unfoldb[:, lanes]
+        cycle_sum = (
+            jnp.dot(hi, table, preferred_element_type=F32)
+            + jnp.dot(mid, table, preferred_element_type=F32)
+        ) + jnp.dot(low, table, preferred_element_type=F32)
+        divisor = e_here + evirt_ref[:, lanes] - e_slab - e_col
+        value = (drive_ref[:, lanes].astype(F32) + cycle_sum) / divisor
+        out[0, :, 0, lanes] = jnp.where(cls == flip(vrow[:, lanes], slab_irr + col_irr), value, 0.0)
 
     def finish(n, carry):
         for o in (1, 2, 3):
@@ -482,38 +563,20 @@
     lax.fori_loop(0, 2, finish_half, 0)
 
 
-def folded_cycle(amplitudes, cycle_block, occ_irrep, virt_irrep, slab_irrep, col_irrep_here, rank_half, rank_all):
-    x = lax.axis_index("occ")
-    v = lax.axis_index("virt")
-    y, z, core = v // 8, (v // 2) % 4, v % 2
-    slab = slab_irrep[0]
-    amp = amplitudes.reshape(25, 32, 1024)
-    wraw = jnp.transpose(cycle_block, (1, 2, 0, 3)).reshape(3200, 1024)
-    vi = virt_irrep.reshape(4, 4, 2, 2, 16)
-    half_cls = jnp.transpose(vi, (3, 1, 2, 0, 4)).reshape(2, 1, 512).astype(F32)
-    mine = lax.dynamic_slice(vi, (0, z, core, 0, 0), (4, 1, 1, 2, 16)).reshape(4, 2, 16)
-    row_par = jnp.transpose(mine, (1, 0, 2)).reshape(2, 64)
-    c_mid = lax.dynamic_slice_in_dim(virt_irrep, 256 * y, 256)
-    two = jnp.arange(2, dtype=jnp.int32)
-    amask = (
-        (slab + two[None, :, None, None] + row_par[:, None, :, None] + c_mid[None, None, None, :]) % 2 == 0
-    ).astype(BF)
-    c_here = lax.dynamic_slice_in_dim(virt_irrep, 32 * v, 32)
-    wmask = (
-        (two[:, None, None] + c_here[None, :, None] + virt_irrep[None, None, :] + col_irrep_here) % 2 == 0
-    ).astype(BF)
-    kk = occ_irrep.reshape(4, 25)
-    main = (kk[:, :24, None] + c_here[None, None, :] + slab).reshape(4, 3, 256)
-    last = jnp.broadcast_to(kk[:, 24:, None, None] + c_here[None, None, None, :] + slab, (4, 1, 8, 32)).reshape(4, 1, 256)
-    lclass = (jnp.concatenate([main, last], axis=1) % 2).reshape(16, 1, 256).astype(F32)
-
+def folded_update(amp, wraw, drive, occ_irrep, virt_irrep, slab_occ, col_occ, occ_energy, virt_energy):
     dma = pltpu.SemaphoreType.DMA
     vmem = pl.BlockSpec(memory_space=pltpu.VMEM)
     hbm = pl.BlockSpec(memory_space=pl.ANY)
     scratch = [
         pltpu.VMEM((3200, 1024), BF),
         pltpu.VMEM((3200, MCAP), BF),
-        pltpu.VMEM((8, 128), BF),
+        pltpu.VMEM((2, 2, 64, 256), BF),
+        pltpu.VMEM((2, 32, 1024), BF),
+        pltpu.VMEM((1, 1024), F32),
+        pltpu.VMEM((1024, 128), F32),
+        pltpu.VMEM((1, 128), F32),
+        pltpu.VMEM((1024, 128), F32),
+        pltpu.VMEM((2, 512, 128), F32),
         pltpu.VMEM((2, CAPL, 512), BF),
         pltpu.VMEM((2, 512, CAPL), BF),
         pltpu.VMEM((1024, MCAP), BF),
@@ -533,6 +596,7 @@
         pltpu.VMEM((2, 2, 3, 4, 8, MCAP), F32),
         pltpu.VMEM((2, 2, 3, 8, MCAP), F32),
         pltpu.VMEM((2, 2, 8, MCAP), F32),
+        pltpu.VMEM((128, 128), F32),
         dma((4,)),
         dma((NSTEP, 3)), dma((NSTEP, 3)), dma((NSTEP,)),
         dma((2, 3)), dma((2, 3)), dma((2,)),
@@ -545,22 +609,16 @@
     ]
     return pl.pallas_call(
         kernel,
-        out_shape=jax.ShapeDtypeStruct((32, 1024), F32),
-        in_specs=[pl.BlockSpec(memory_space=pltpu.SMEM), hbm, hbm] + [vmem] * 6,
+        out_shape=jax.ShapeDtypeStruct(OUT, F32),
+        in_specs=[pl.BlockSpec(memory_space=pltpu.SMEM)] * 4 + [vmem] * 3 + [hbm, hbm],
         out_specs=vmem,
         scratch_shapes=scratch,
         compiler_params=pltpu.CompilerParams(
             collective_id=0, has_side_effects=True, vmem_limit_bytes=52 * 2**20
         ),
         name="cycle",
-    )(occ_irrep, amp, wraw, rank_half, half_cls, rank_all, amask, wmask, lclass)
-
-
-def ranks(cls):
-    n = cls.shape[-1]
-    same = cls[..., :, None] == cls[..., None, :]
-    before = jnp.arange(n)[:, None] < jnp.arange(n)[None, :]
-    return jnp.sum(jnp.where(same & before, 1, 0), axis=-2, dtype=jnp.int32)
+    )(occ_irrep, slab_occ, col_occ, occ_energy, virt_irrep.reshape(1, 1024), virt_energy.reshape(1, 1024),
+      drive, amp, wraw)
 
 
 def body(
@@ -574,46 +632,20 @@
     slab_occ,
     col_occ,
 ):
-    a_cols = amplitudes.shape[2]
-    j_cols = cycle_block.shape[2]
-    occ_pos = lax.axis_index("occ")
-    virt_pos = lax.axis_index("virt")
-    slab_irrep = pick_entries(occ_irrep, slab_occ)
-    col_irrep = pick_entries(occ_irrep, col_occ)
-    irr_a = lax.dynamic_slice_in_dim(virt_irrep, virt_pos * a_cols, a_cols)
-    irr_cols = lax.dynamic_slice_in_dim(col_irrep, occ_pos * j_cols, j_cols)
-
-    half = jnp.transpose(virt_irrep.reshape(4, 4, 2, 2, 16), (3, 1, 2, 0, 4)).reshape(2, 512)
-    rank_half = ranks(half)
-    rank_all = ranks(virt_irrep)
-    fits = jnp.logical_and(jnp.max(rank_half) < CAP, jnp.max(rank_all) < MCAP)
-
-    cycle_sum = lax.cond(
-        fits,
-        lambda *args: folded_cycle(*args),
-        lambda amp, w, occ, virt, slab, *rest: general_cycle(amp, w, occ, virt, slab),
-        amplitudes, cycle_block, occ_irrep, virt_irrep, slab_irrep, irr_cols[0],
-        rank_half.reshape(2, 1, 512).astype(F32), rank_all.reshape(1, 1024).astype(F32),
+    amp = amplitudes.reshape(25, 32, 1024)
+    wraw = jnp.transpose(cycle_block, (1, 2, 0, 3)).reshape(3200, 1024)
+    drive = jnp.transpose(drive_term, (0, 2, 1, 3)).reshape(32, 1024)
+    half = (jnp.arange(1024, dtype=jnp.int32) // 16) % 2
+    count = jnp.sum(virt_irrep * jnp.where(half == 0, 1, 4096))
+    first, second = count % 4096, count // 4096
+    fits = (
+        (first <= CAP) & (first >= 512 - CAP) & (second <= CAP) & (second >= 512 - CAP)
+        & (first + second <= MCAP) & (first + second >= 1024 - MCAP)
     )
-    cycle_sum = cycle_sum.reshape(1, a_cols, j_cols, 1024)
-
-    e_slab = pick_entries(occ_energy, slab_occ)
-    e_cols = lax.dynamic_slice_in_dim(pick_entries(occ_energy, col_occ), occ_pos * j_cols, j_cols)
-    e_rows = lax.dynamic_slice_in_dim(virt_energy, virt_pos * a_cols, a_cols)
-    divisor = (
-        e_rows[None, :, None, None]
-        + virt_energy[None, None, None, :]
-        - e_slab[:, None, None, None]
-        - e_cols[None, None, :, None]
+    return lax.cond(
+        fits, folded_update, general_update,
+        amp, wraw, drive, occ_irrep, virt_irrep, slab_occ, col_occ, occ_energy, virt_energy,
     )
-    out_parity = (
-        slab_irrep[:, None, None, None]
-        + irr_a[None, :, None, None]
-        + irr_cols[None, None, :, None]
-        + virt_irrep[None, None, None, :]
-    )
-    value = (drive_term.astype(jnp.float32) + cycle_sum) / divisor
-    return jnp.where(out_parity % 2 == 0, value, jnp.zeros((), jnp.float32))
 
 
 def solution(mesh):

time: 111 us -> 81.5 us (0.73)
  other arithmetic: 14.9 us -> 1.33 us
  between operations: 15.4 us -> 2.64 us
  local copies, waits for them, and re-layouts: 6.21 us -> 0.66 us
  Pallas kernels: 74 us -> 76.4 us
    add x6 -> x0, other arithmetic: 4.28 us -> none  [the longest x1 2.06 us: body(): slab_irrep[:, None, None, None] + irr_a[None, :, None, None]]
    reduce_sum x6 -> x1, other arithmetic: 4.81 us -> 1.33 us  [body(): count = jnp.sum(virt_irrep * jnp.where(half == 0, 1, 4096))]
    dynamic_slice x5 -> x0, local copies, waits for them, and re-layouts: 2.89 us -> none  [the longest x1 0.76 us: folded_cycle(): c_here = lax.dynamic_slice_in_dim(virt_irrep, 32 * v, 32)]
    select_n x1 -> x0, other arithmetic: 2.65 us -> none  [body(): return jnp.where(out_parity % 2 == 0, value, jnp.zeros((), jnp.float32))]
    pallas_call x1, Pallas kernels: 74 us -> 76.4 us  [folded_update(): pl.pallas_call(kernel, out_shape=jax.ShapeDtypeStruct(OUT, F32), in_specs...]
    reshape x3 -> x0, local copies, waits for them, and re-layouts: 2.3 us -> none  [the longest x1 0.78 us: folded_cycle(): vi = virt_irrep.reshape(4, 4, 2, 2, 16)]
    convert_element_type x6 -> x0, other arithmetic: 1.76 us -> none  [the longest x1 1.5 us: folded_cycle(): wmask = ((two[:, None, None] + c_here[None, :, None] + virt_irrep[None, N...]
    reduce_max x2 -> x0, other arithmetic: 1.28 us -> none  [body(): fits = jnp.logical_and(jnp.max(rank_half) < CAP, jnp.max(rank_all) < MCAP)]
where the time goes in v2:
time: 81.5 us; the launch traced here: 81.2 us
  Pallas kernels  76.4 us (94%)
  between operations  2.64 us (3%)
  other arithmetic  1.33 us (2%)
    pallas_call x1, Pallas kernels, folded_update(): pl.pallas_call(kernel, out_shape=jax.ShapeDtypeStruct(OUT, F32), in_specs...  76.4 us

profile of v2, /device:TPU:1, one launch (start us, length us, event | category | flops | bytes accessed | tf_op | source)
XLA Modules:
  0.0 81.2 jit_solution(10537510166322242005)
XLA Ops:
  0.0 1.3 %multiply_reduce_fusion = s32[]{:T(128)} fusion(s32[1024]{0:T(1024)} %param.17), kind=kLoop, calls=%fused_computation.42 | loop fusion | flops 23551 | bytes 4100 | tf_op jit(solution)/shard_map/reduce_sum | solution.py:639
  4.0 76.6 %conditional.1 = (f32[1,32,1,1024]{3,2,1,0:T(1,128)S(1)}) conditional(s32[]{:T(128)} %convert_element_type.6, (s32[1]{0:T(128)}, s32[100]{0:T(128)}, s32[1024]{0:T(1024)}, s32[4]{0:T(128)}, bf16[32,1024]{1,0:T(8,128)(2,1)}, /*index=5*/bf16[25,32,1024]{2,1,0:T(8,128)(2,1)}, bf16[100,1,32,1024]{3,2,0,1:T(8,128)(2,1)}, f32[1024]{0:T(1024)}, ...), branch_computations={%region_1.7_spmd, %region_7.8_spmd} | conditional | flops 6724028416 | bytes 105568600 | solution.py:645
  4.2 76.4 %cycle.1 = f32[1,32,1,1024]{3,2,1,0:T(1,128)S(1)} custom-call(s32[100]{0:T(128)} %get-tuple-element.53.occ_ref, s32[1]{0:T(128)} %get-tuple-element.54.slab_ref, s32[4]{0:T(128)} %get-tuple-element.55.colo_ref, f32[100]{0:T(128)} %get-tuple-element.56.eocc_ref, s32[1,1024]{1,0:T(1,128)} %bitcast.42, f32[1,1024]{1,0:T(1,128)} %bitcast.43, ...), custom_call_target="tpu_custom_call" | custom-call | tf_op jit(solution)/shard_map/cond/branch_1_fun/cycle/pallas_call | solution.py:610
  80.5 0.7 copy.60

commit v3 on v2

--- a/solution.py
+++ b/solution.py
@@ -11,6 +11,7 @@
 MCAP = 640
 NSTEP = 6
 OUT = (1, 32, 1, 1024)
+GL = 1
 BF = jnp.bfloat16
 F32 = jnp.float32
 
@@ -67,7 +68,7 @@
 def kernel(
     occ_ref, slab_ref, colo_ref, eocc_ref, virt_ref, evirt_ref, drive_ref, amp, wraw,
     out,
-    wv, wf, amask, wmask, vrow, col, crow, rankb, rankh, fold, unfold, foldb, unfoldb, clsb, mbuf, sbuf, sleft, abuf, aleft,
+    wv, wf, wrep, wide, widel, amask, wmask, vrow, col, crow, rankb, rankh, fold, unfold, foldb, unfoldb, clsb, mbuf, sbuf, sleft, abuf, aleft,
     xbuf, xleft, zacc, crecv, tsum, t2, r1buf, r2buf, fin, ecol,
     wsem, ysend, yrecv, yloc, ysendl, yrecvl, ylocl,
     zsend, zrecv, zloc, zsendl, zrecvl, zlocl,
@@ -196,7 +197,7 @@
         for o in (2, 1, 3):
             y_copy(n, o).start()
         y_own(n).start()
-        if n % 3 == 2:
+        if n % 3 == GL:
             for o in (2, 1, 3):
                 y_copyl(n // 3, o).start()
             y_ownl(n // 3).start()
@@ -282,14 +283,24 @@
             row = jnp.where(lane128 // 32 == q, other, row)
         return row
 
-    def prepare_w(j, carry):
+    def prepare_w(i):
+        w_copy(i).wait()
+
+        def mask_k(k, carry):
+            rows = pl.ds(pl.multiple_of(800 * i + 32 * k, 32), 32)
+            wv[rows, :] = wv[rows, :] * wmask[occ_ref[25 * i + k]]
+            return carry
+
+        lax.fori_loop(0, 25, mask_k, 0, unroll=5)
+        rows = pl.ds(pl.multiple_of(800 * i, 32), 800)
+        value = jnp.dot(wv[rows, :], foldb[...], preferred_element_type=F32).astype(BF)
+        for g in range(3):
+            wf[g, i] = value[256 * g:256 * g + 256]
         for q in range(4):
-            par = occ_ref[4 * j + q]
-            rows = pl.ds(pl.multiple_of(128 * j + 32 * q, 32), 32)
-            wv[rows, :] = wv[rows, :] * wmask[par]
-        rows = pl.ds(pl.multiple_of(128 * j, 128), 128)
-        wf[rows, :] = jnp.dot(wv[rows, :], foldb[...], preferred_element_type=F32).astype(BF)
-        return carry
+            wrep[i, q] = value[768:800]
+
+    rank_tables()
+    more_tables()
 
     def relay(n):
         h, g = n // 3, n % 3
@@ -312,7 +323,7 @@
             z_copy(n, o).start()
         z_own(n).start()
 
-        @pl.when(g == 2)
+        @pl.when(g == GL)
         def _():
             for o in (1, 2, 3):
                 y_copyl(h, o).wait_recv()
@@ -337,7 +348,7 @@
         for side in range(2):
             x_copy(n, side).start()
 
-        @pl.when(g == 2)
+        @pl.when(g == GL)
         def _():
             for o in range(1, 8):
                 z_copyl(h, o).wait_recv()
@@ -358,34 +369,27 @@
             for side in range(2):
                 x_copyl(h, side).start()
 
-    def product(n, slot):
+    def spread(n, slot):
         h, g = n // 3, n % 3
         src = (x + (0, 3, 1, 2)[slot]) % 4
         part = jnp.dot(unfold[h, :, :CAP], xbuf[n, slot], preferred_element_type=F32)
         cls = clsb[h]
-        part = jnp.concatenate(
-            [jnp.where(cls == lane_class(src, 8 * g + 4 * t, 1), part[:, 128 * t:128 * t + 128], 0.0)
-             for t in range(2)], axis=1).astype(BF)
-        rows = pl.ds(pl.multiple_of(800 * src + 256 * g, 32), 256)
-        value = jnp.dot(part, wf[rows, :], preferred_element_type=F32)
-        for zz in range(4):
-            for cc in range(2):
-                r0 = (zz * 2 + cc) * 64
-                zacc[h, zz, cc] += value[r0:r0 + 64]
-
-    def product_left(h, slot):
+        for t in range(2):
+            piece = jnp.where(
+                cls == lane_class(src, 8 * g + 4 * t, 1), part[:, 128 * t:128 * t + 128], 0.0).astype(BF)
+            for i in range(8):
+                wide[n % 2, i // 2, i % 2, :, pl.ds(pl.multiple_of(256 * src + 128 * t, 128), 128)] = (
+                    piece[64 * i:64 * i + 64])
+
+    def spread_left(h, slot):
         src = (x + (0, 3, 1, 2)[slot]) % 4
         got = xleft[h, slot].astype(F32)
-        spread = jnp.concatenate(
+        stacked = jnp.concatenate(
             [jnp.where(lane128 // 32 == q, got, 0.0) for q in range(4)], axis=0).astype(BF)
-        part = jnp.dot(unfold[h], spread, preferred_element_type=F32)
+        part = jnp.dot(unfold[h], stacked, preferred_element_type=F32)
         part = jnp.where(clsb[h] == lane_class(src, 24, 0), part, 0.0).astype(BF)
-        one = wf[pl.ds(pl.multiple_of(800 * src + 768, 32), 32), :]
-        value = jnp.dot(part, jnp.concatenate([one] * 4, axis=0), preferred_element_type=F32)
-        for zz in range(4):
-            for cc in range(2):
-                r0 = (zz * 2 + cc) * 64
-                zacc[h, zz, cc] += value[r0:r0 + 64]
+        for i in range(8):
+            widel[h, i // 2, i % 2, :, pl.ds(pl.multiple_of(128 * src, 128), 128)] = part[64 * i:64 * i + 64]
 
     def near_step(n):
         h, g = n // 3, n % 3
@@ -393,7 +397,7 @@
             x_copy(n, side).wait_recv()
             f_copy(n, side).start()
 
-        @pl.when(g == 2)
+        @pl.when(g == GL)
         def _():
             for side in range(2):
                 x_copyl(h, side).wait_recv()
@@ -406,29 +410,48 @@
             def _():
                 f_copyl(h, 1).start()
 
+        for slot in range(3):
+            spread(n, slot)
+
+        @pl.when(g == GL)
+        def _():
+            for slot in range(3):
+                spread_left(h, slot)
+
+    def product(n, cc):
+        h, g = n // 3, n % 3
+        left_side = wide[n % 2, :, cc].reshape(256, 1024)
+        value = jnp.dot(left_side, wf[g].reshape(1024, MCAP), preferred_element_type=F32).reshape(4, 64, MCAP)
+
         @pl.when(g == 0)
         def _():
-            zacc[h] = jnp.zeros_like(zacc[h])
-
-        for slot in range(3):
-            product(n, slot)
-
-        @pl.when(g == 2)
-        def _():
-            for slot in range(3):
-                product_left(h, slot)
+            zacc[h, :, cc] = value
+
+        @pl.when(g > 0)
+        def _():
+            zacc[h, :, cc] += value
 
     def far_step(n):
         h, g = n // 3, n % 3
         for side in range(2):
             f_copy(n, side).wait_recv()
-        product(n, 3)
+        spread(n, 3)
+        product(n, 1 - core)
 
         @pl.when(g == 2)
         def _():
+            c_copy(h).start()
+
+        product(n, core)
+
+        @pl.when(g == GL)
+        def _():
             f_copyl(h, 0).wait_recv()
-            product_left(h, 3)
-            c_copy(h).start()
+            spread_left(h, 3)
+            table = wrep[...].reshape(512, MCAP)
+            for cc in range(2):
+                zacc[h, :, cc] += jnp.dot(
+                    widel[h, :, cc].reshape(256, 512), table, preferred_element_type=F32).reshape(4, 64, MCAP)
 
     def sum_core(h):
         c_copy(h).wait_recv()
@@ -467,7 +490,8 @@
 
         @pl.when(n == 0)
         def _():
-            rank_tables()
+            prepare_w(0)
+            prepare_w(1)
 
         @pl.when(jnp.logical_and(n >= 1, n < NSTEP + 1))
         def _():
@@ -475,14 +499,8 @@
 
         @pl.when(n == 1)
         def _():
-            more_tables()
-            for i in range(4):
-                w_copy(i).wait()
-            lax.fori_loop(0, 9, prepare_w, 0)
-
-        @pl.when(n == 2)
-        def _():
-            lax.fori_loop(9, 25, prepare_w, 0)
+            prepare_w(2)
+            prepare_w(3)
 
         @pl.when(n == 3)
         def _():
@@ -569,7 +587,10 @@
     hbm = pl.BlockSpec(memory_space=pl.ANY)
     scratch = [
         pltpu.VMEM((3200, 1024), BF),
-        pltpu.VMEM((3200, MCAP), BF),
+        pltpu.VMEM((3, 4, 256, MCAP), BF),
+        pltpu.VMEM((4, 4, 32, MCAP), BF),
+        pltpu.VMEM((2, 4, 2, 64, 1024), BF),
+        pltpu.VMEM((2, 4, 2, 64, 512), BF),
         pltpu.VMEM((2, 2, 64, 256), BF),
         pltpu.VMEM((2, 32, 1024), BF),
         pltpu.VMEM((1, 1024), F32),

time: 81.5 us -> 79.1 us (0.971)
  Pallas kernels: 76.4 us -> 74 us
    pallas_call x1, Pallas kernels: 76.4 us -> 74 us  [folded_update(): pl.pallas_call(kernel, out_shape=jax.ShapeDtypeStruct(OUT, F32), in_specs...]
where the time goes in v3:
time: 79.1 us; the launch traced here: 78.9 us
  Pallas kernels  74 us (94%)
  between operations  2.64 us (3%)
  other arithmetic  1.33 us (2%)
    pallas_call x1, Pallas kernels, folded_update(): pl.pallas_call(kernel, out_shape=jax.ShapeDtypeStruct(OUT, F32), in_specs...  74 us

profile of v3, /device:TPU:1, one launch (start us, length us, event | category | flops | bytes accessed | tf_op | source)
XLA Modules:
  0.0 78.9 jit_solution(7746058598499660130)
XLA Ops:
  0.0 1.3 %multiply_reduce_fusion = s32[]{:T(128)} fusion(s32[1024]{0:T(1024)} %param.17), kind=kLoop, calls=%fused_computation.42 | loop fusion | flops 23551 | bytes 4100 | tf_op jit(solution)/shard_map/reduce_sum | solution.py:660
  4.0 74.3 %conditional.1 = (f32[1,32,1,1024]{3,2,1,0:T(1,128)S(1)}) conditional(s32[]{:T(128)} %convert_element_type.6, (s32[1]{0:T(128)}, s32[100]{0:T(128)}, s32[1024]{0:T(1024)}, s32[4]{0:T(128)}, bf16[32,1024]{1,0:T(8,128)(2,1)}, /*index=5*/bf16[25,32,1024]{2,1,0:T(8,128)(2,1)}, bf16[100,1,32,1024]{3,2,0,1:T(8,128)(2,1)}, f32[1024]{0:T(1024)}, ...), branch_computations={%region_1.7_spmd, %region_7.8_spmd} | conditional | flops 6724028416 | bytes 105568600 | solution.py:666
  4.0 74.0 %cycle.1 = f32[1,32,1,1024]{3,2,1,0:T(1,128)S(1)} custom-call(s32[100]{0:T(128)} %get-tuple-element.53.occ_ref, s32[1]{0:T(128)} %get-tuple-element.54.slab_ref, s32[4]{0:T(128)} %get-tuple-element.55.colo_ref, f32[100]{0:T(128)} %get-tuple-element.56.eocc_ref, s32[1,1024]{1,0:T(1,128)} %bitcast.42, f32[1,1024]{1,0:T(1,128)} %bitcast.43, ...), custom_call_target="tpu_custom_call" | custom-call | tf_op jit(solution)/shard_map/cond/branch_1_fun/cycle/pallas_call | solution.py:631
  78.2 0.7 copy.60

commit v4 on v3

--- a/solution.py
+++ b/solution.py
@@ -66,11 +66,12 @@
 
 
 def kernel(
-    occ_ref, slab_ref, colo_ref, eocc_ref, virt_ref, evirt_ref, drive_ref, amp, wraw,
-    out,
+    occ_in, slab_in, colo_in, eocc_in, virt_in, evirt_in, drive_in, amp, wraw,
+    out, fits_ref,
+    occ_ref, slab_ref, colo_ref, eocc_ref, virt_ref, evirt_ref, drive_ref,
     wv, wf, wrep, wide, widel, amask, wmask, vrow, col, crow, rankb, rankh, fold, unfold, foldb, unfoldb, clsb, mbuf, sbuf, sleft, abuf, aleft,
     xbuf, xleft, zacc, crecv, tsum, t2, r1buf, r2buf, fin, ecol,
-    wsem, ysend, yrecv, yloc, ysendl, yrecvl, ylocl,
+    insem, wsem, ysend, yrecv, yloc, ysendl, yrecvl, ylocl,
     zsend, zrecv, zloc, zsendl, zrecvl, zlocl,
     xsend, xrecv, fsend, frecv, xsendl, xrecvl, fsendl, frecvl,
     csend, crecvs, r1send, r1recv, r2send, r2recv,
@@ -182,6 +183,15 @@
         yd = (y + o) % 4
         return remote(t2.at[h, 1, yd], r2buf.at[h, 1, o - 1], r2send.at[h, 2 + o],
                       r2recv.at[h, 2 + o], (x, virt_at(yd, z, core)))
+
+    loads = [
+        pltpu.make_async_copy(src, dst, insem.at[i])
+        for i, (src, dst) in enumerate((
+            (occ_in, occ_ref), (slab_in, slab_ref), (colo_in, colo_ref), (eocc_in, eocc_ref),
+            (virt_in, virt_ref), (evirt_in, evirt_ref), (drive_in, drive_ref)))
+    ]
+    for load in loads:
+        load.start()
 
     barrier = pltpu.get_barrier_semaphore()
     peers = [y_peer(o) for o in (1, 2, 3)] + [z_peer(o) for o in range(1, 8)] + [(right, v), (left, v)]
@@ -207,6 +217,8 @@
 
     lane128 = lax.broadcasted_iota(jnp.int32, (1, 128), 1)
 
+    for load in loads:
+        load.wait()
     slab = slab_ref[0]
     slab_irr = occ_ref[slab]
     colo = colo_ref[x]
@@ -220,6 +232,15 @@
 
     vrow[...] = virt_ref[...].astype(F32)
     col[...] = jnp.transpose(jnp.broadcast_to(vrow[...], (128, 1024)))
+    second = (lax.broadcasted_iota(jnp.int32, (1, 1024), 1) & 16) != 0
+    ones_b = jnp.sum(jnp.where(second, vrow[...], 0.0))
+    ones_a = jnp.sum(vrow[...]) - ones_b
+    total = ones_a + ones_b
+    fits = (
+        (ones_a <= CAP) & (ones_a >= 512 - CAP) & (ones_b <= CAP) & (ones_b >= 512 - CAP)
+        & (total <= MCAP) & (total >= 1024 - MCAP)
+    )
+    fits_ref[0] = fits.astype(jnp.int32)
     for h in range(2):
         rows = jnp.concatenate(
             [col[pl.ds(pl.multiple_of(256 * yy + 32 * (me8) + 16 * h, 16), 16), :] for yy in range(4)], axis=0)
@@ -500,27 +521,30 @@
         @pl.when(n == 1)
         def _():
             prepare_w(2)
+
+        @pl.when(n == 3)
+        def _():
+            last_tables()
+
+        @pl.when(jnp.logical_and(n >= 2, n < NSTEP + 2))
+        def _():
+            near_step(n - 2)
+
+        @pl.when(n == 2)
+        def _():
             prepare_w(3)
 
-        @pl.when(n == 3)
-        def _():
-            last_tables()
-
-        @pl.when(jnp.logical_and(n >= 2, n < NSTEP + 2))
-        def _():
-            near_step(n - 2)
-
         @pl.when(jnp.logical_or(n == 6, n == 9))
         def _():
             sum_core(n // 3 - 2)
 
+        @pl.when(jnp.logical_and(n >= 3, n < NSTEP + 3))
+        def _():
+            far_step(n - 3)
+
         @pl.when(jnp.logical_or(n == 7, n == 10))
         def _():
             sum_first(n // 3 - 2)
-
-        @pl.when(jnp.logical_and(n >= 3, n < NSTEP + 3))
-        def _():
-            far_step(n - 3)
 
         return carry
 
@@ -585,7 +609,10 @@
     dma = pltpu.SemaphoreType.DMA
     vmem = pl.BlockSpec(memory_space=pltpu.VMEM)
     hbm = pl.BlockSpec(memory_space=pl.ANY)
+    smem = pltpu.SMEM
     scratch = [
+        smem((100,), jnp.int32), smem((1,), jnp.int32), smem((4,), jnp.int32), smem((100,), F32),
+        pltpu.VMEM((1, 1024), jnp.int32), pltpu.VMEM((1, 1024), F32), pltpu.VMEM((32, 1024), BF),
         pltpu.VMEM((3200, 1024), BF),
         pltpu.VMEM((3, 4, 256, MCAP), BF),
         pltpu.VMEM((4, 4, 32, MCAP), BF),
@@ -618,7 +645,7 @@
         pltpu.VMEM((2, 2, 3, 8, MCAP), F32),
         pltpu.VMEM((2, 2, 8, MCAP), F32),
         pltpu.VMEM((128, 128), F32),
-        dma((4,)),
+        dma((7,)), dma((4,)),
         dma((NSTEP, 3)), dma((NSTEP, 3)), dma((NSTEP,)),
         dma((2, 3)), dma((2, 3)), dma((2,)),
         dma((NSTEP, 7)), dma((NSTEP, 7)), dma((NSTEP,)),
@@ -630,12 +657,12 @@
     ]
     return pl.pallas_call(
         kernel,
-        out_shape=jax.ShapeDtypeStruct(OUT, F32),
-        in_specs=[pl.BlockSpec(memory_space=pltpu.SMEM)] * 4 + [vmem] * 3 + [hbm, hbm],
-        out_specs=vmem,
+        out_shape=(jax.ShapeDtypeStruct(OUT, F32), jax.ShapeDtypeStruct((1,), jnp.int32)),
+        in_specs=[hbm] * 9,
+        out_specs=(vmem, pl.BlockSpec(memory_space=smem)),
         scratch_shapes=scratch,
         compiler_params=pltpu.CompilerParams(
-            collective_id=0, has_side_effects=True, vmem_limit_bytes=52 * 2**20
+            collective_id=0, has_side_effects=True, vmem_limit_bytes=56 * 2**20
         ),
         name="cycle",
     )(occ_irrep, slab_occ, col_occ, occ_energy, virt_irrep.reshape(1, 1024), virt_energy.reshape(1, 1024),
@@ -656,17 +683,10 @@
     amp = amplitudes.reshape(25, 32, 1024)
     wraw = jnp.transpose(cycle_block, (1, 2, 0, 3)).reshape(3200, 1024)
     drive = jnp.transpose(drive_term, (0, 2, 1, 3)).reshape(32, 1024)
-    half = (jnp.arange(1024, dtype=jnp.int32) // 16) % 2
-    count = jnp.sum(virt_irrep * jnp.where(half == 0, 1, 4096))
-    first, second = count % 4096, count // 4096
-    fits = (
-        (first <= CAP) & (first >= 512 - CAP) & (second <= CAP) & (second >= 512 - CAP)
-        & (first + second <= MCAP) & (first + second >= 1024 - MCAP)
-    )
-    return lax.cond(
-        fits, folded_update, general_update,
-        amp, wraw, drive, occ_irrep, virt_irrep, slab_occ, col_occ, occ_energy, virt_energy,
-    )
+    amp, wraw, drive = lax.optimization_barrier((amp, wraw, drive))
+    args = (amp, wraw, drive, occ_irrep, virt_irrep, slab_occ, col_occ, occ_energy, virt_energy)
+    folded, fits = folded_update(*args)
+    return lax.cond(fits[0] == 1, lambda value, *rest: value, lambda value, *rest: general_update(*rest), folded, *args)
 
 
 def solution(mesh):

time: 79.1 us -> 74.5 us (0.942)
  Pallas kernels: 74 us -> 72.4 us
  other arithmetic: 1.33 us -> 0 us
  between operations: 2.64 us -> 1.34 us
    pallas_call x1, Pallas kernels: 74 us -> 72.4 us  [folded_update(): pl.pallas_call(kernel, out_shape=(jax.ShapeDtypeStruct(OUT, F32), jax.Sha...]
    reduce_sum x1 -> x0, other arithmetic: 1.33 us -> none  [body(): count = jnp.sum(virt_irrep * jnp.where(half == 0, 1, 4096))]
where the time goes in v4:
time: 74.5 us; the launch traced here: 74.4 us
  Pallas kernels  72.4 us (97%)
  between operations  1.34 us (2%)
    pallas_call x1, Pallas kernels, folded_update(): pl.pallas_call(kernel, out_shape=(jax.ShapeDtypeStruct(OUT, F32), jax.Sha...  72.4 us

profile of v4, /device:TPU:1, one launch (start us, length us, event | category | flops | bytes accessed | tf_op | source)
XLA Modules:
  0.0 74.4 jit_solution(15962140028799682686)
XLA Ops:
  0.7 0.0 copy-start
  0.7 0.0 copy-start.1
  0.7 0.0 copy-start.2
  0.7 0.0 copy-start.3
  0.7 0.0 copy-start.4
  0.7 0.0 copy-start.5
  0.7 0.0 copy-start.6
  0.7 72.4 %cycle.1 = (f32[1,32,1,1024]{3,2,1,0:T(1,128)S(1)}, s32[1]{0:T(128)}) custom-call(s32[100]{0:T(128)} %occ_in.1, s32[1]{0:T(128)S(6)} %copy.46.slab_in, s32[4]{0:T(128)} %colo_in.1, f32[100]{0:T(128)} %eocc_in.1, s32[1,1024]{1,0:T(1,128)} %bitcast.38, f32[1,1024]{1,0:T(1,128)} %bitcast.39, bf16[32,1024]{1,0:T(8,128)(2,1)} %bitcast.36, ...), custom_call_target="tpu_custom_call" | custom-call | tf_op jit(solution)/shard_map/cycle/pallas_call | solution.py:658
  73.7 0.0 copy-done
  73.7 0.0 copy-done.1
  73.7 0.0 copy-done.2
  73.7 0.0 copy-done.3
  73.7 0.0 copy-done.4
  73.7 0.0 copy-done.5
  73.7 0.0 copy-done.6
  73.8 0.7 copy.47
  (1 shorter events, 0.0 us)
Async XLA Ops:
  0.7 73.0 %copy-start = (bf16[1,25,32,1024]{3,2,1,0:T(8,128)(2,1)S(1)}, bf16[1,25,32,1024]{3,2,1,0:T(8,128)(2,1)}, u32[]{:S(2)}) copy-start(bf16[1,25,32,1024]{3,2,1,0:T(8,128)(2,1)} %param.11) | copy-start | bytes 4915204
  0.7 73.0 %copy-start.1 = (bf16[1,32,1,1024]{3,1,2,0:T(8,128)(2,1)S(1)}, bf16[1,32,1,1024]{3,1,2,0:T(8,128)(2,1)}, u32[]{:S(2)}) copy-start(bf16[1,32,1,1024]{3,1,2,0:T(8,128)(2,1)} %param.13) | copy-start | bytes 196612
  0.7 73.0 %copy-start.2 = (s32[1024]{0:T(1024)S(1)}, s32[1024]{0:T(1024)}, u32[]{:S(2)}) copy-start(s32[1024]{0:T(1024)} %param.17) | copy-start | bytes 12292
  0.7 73.0 %copy-start.3 = (f32[1024]{0:T(1024)S(1)}, f32[1024]{0:T(1024)}, u32[]{:S(2)}) copy-start(f32[1024]{0:T(1024)} %param.15) | copy-start | bytes 12292
  0.7 73.0 %copy-start.4 = (s32[100]{0:T(128)S(1)}, s32[100]{0:T(128)}, u32[]{:S(2)}) copy-start(s32[100]{0:T(128)} %occ_in.1) | copy-start | bytes 1204
  0.7 73.0 %copy-start.5 = (f32[100]{0:T(128)S(1)}, f32[100]{0:T(128)}, u32[]{:S(2)}) copy-start(f32[100]{0:T(128)} %eocc_in.1) | copy-start | bytes 1204
  0.7 73.0 %copy-start.6 = (s32[4]{0:T(128)S(1)}, s32[4]{0:T(128)}, u32[]{:S(2)}) copy-start(s32[4]{0:T(128)} %colo_in.1) | copy-start | bytes 52

commit v5 on v4

--- a/solution.py
+++ b/solution.py
@@ -504,6 +504,8 @@
         fin[h, 0] = t2[h, 0, z] + r2buf[h, 0, 0] + r2buf[h, 0, 1] + r2buf[h, 0, 2]
         fin[h, 1] = t2[h, 1, y] + r2buf[h, 1, 0] + r2buf[h, 1, 1] + r2buf[h, 1, 2]
 
+    prepare_w(0)
+
     def step(n, carry):
         @pl.when(n < NSTEP)
         def _():
@@ -511,7 +513,6 @@
 
         @pl.when(n == 0)
         def _():
-            prepare_w(0)
             prepare_w(1)
 
         @pl.when(jnp.logical_and(n >= 1, n < NSTEP + 1))
@@ -542,6 +543,10 @@
         def _():
             far_step(n - 3)
 
+        @pl.when(n == 9)
+        def _():
+            sum_second(0)
+
         @pl.when(jnp.logical_or(n == 7, n == 10))
         def _():
             sum_first(n // 3 - 2)
@@ -549,7 +554,6 @@
         return carry
 
     lax.fori_loop(0, 11, step, 0)
-    sum_second(0)
     sum_second(1)
 
     total = jnp.concatenate([fin[0, 0], fin[0, 1], fin[1, 0], fin[1, 1]], axis=0)
@@ -564,13 +568,11 @@
     e_slab = eocc_ref[slab]
     e_col = eocc_ref[colo]
     cls = col[pl.ds(pl.multiple_of(32 * v, 32), 32), :]
+    parts = jnp.concatenate([hi.astype(F32), mid.astype(F32), low.astype(F32)], axis=0).astype(BF)
+    spread_out = jnp.dot(parts, unfoldb[...], preferred_element_type=F32)
     for t in range(8):
         lanes = slice(128 * t, 128 * t + 128)
-        table = unfoldb[:, lanes]
-        cycle_sum = (
-            jnp.dot(hi, table, preferred_element_type=F32)
-            + jnp.dot(mid, table, preferred_element_type=F32)
-        ) + jnp.dot(low, table, preferred_element_type=F32)
+        cycle_sum = (spread_out[0:32, lanes] + spread_out[32:64, lanes]) + spread_out[64:96, lanes]
         divisor = e_here + evirt_ref[:, lanes] - e_slab - e_col
         value = (drive_ref[:, lanes].astype(F32) + cycle_sum) / divisor
         out[0, :, 0, lanes] = jnp.where(cls == flip(vrow[:, lanes], slab_irr + col_irr), value, 0.0)

time: 74.5 us -> 74.8 us (level)
  no operation moved by 1% of the time
where the time goes in v5:
time: 74.8 us; the launch traced here: 74.7 us
  Pallas kernels  72.4 us (97%)
  between operations  1.34 us (2%)
    pallas_call x1, Pallas kernels, folded_update(): pl.pallas_call(kernel, out_shape=(jax.ShapeDtypeStruct(OUT, F32), jax.Sha...  72.4 us

profile of v5, /device:TPU:1, one launch (start us, length us, event | category | flops | bytes accessed | tf_op | source)
XLA Modules:
  0.0 74.7 jit_solution(1853824939644125012)
XLA Ops:
  0.7 0.0 copy-start
  0.7 0.0 copy-start.1
  0.7 0.0 copy-start.2
  0.7 0.0 copy-start.3
  0.7 0.0 copy-start.4
  0.7 0.0 copy-start.5
  0.7 0.0 copy-start.6
  0.7 72.4 %cycle.1 = (f32[1,32,1,1024]{3,2,1,0:T(1,128)S(1)}, s32[1]{0:T(128)}) custom-call(s32[100]{0:T(128)} %occ_in.1, s32[1]{0:T(128)S(6)} %copy.46.slab_in, s32[4]{0:T(128)} %colo_in.1, f32[100]{0:T(128)} %eocc_in.1, s32[1,1024]{1,0:T(1,128)} %bitcast.38, f32[1,1024]{1,0:T(1,128)} %bitcast.39, bf16[32,1024]{1,0:T(8,128)(2,1)} %bitcast.36, ...), custom_call_target="tpu_custom_call" | custom-call | tf_op jit(solution)/shard_map/cycle/pallas_call | solution.py:660
  73.7 0.0 copy-done
  73.7 0.0 copy-done.1
  73.7 0.0 copy-done.2
  73.7 0.0 copy-done.3
  73.8 0.0 copy-done.4
  73.8 0.0 copy-done.5
  73.8 0.0 copy-done.6
  73.8 0.2 conditional.1
  74.0 0.7 copy.47
Async XLA Ops:
  0.7 73.1 %copy-start = (bf16[1,25,32,1024]{3,2,1,0:T(8,128)(2,1)S(1)}, bf16[1,25,32,1024]{3,2,1,0:T(8,128)(2,1)}, u32[]{:S(2)}) copy-start(bf16[1,25,32,1024]{3,2,1,0:T(8,128)(2,1)} %param.11) | copy-start | bytes 4915204
  0.7 73.1 %copy-start.1 = (bf16[1,32,1,1024]{3,1,2,0:T(8,128)(2,1)S(1)}, bf16[1,32,1,1024]{3,1,2,0:T(8,128)(2,1)}, u32[]{:S(2)}) copy-start(bf16[1,32,1,1024]{3,1,2,0:T(8,128)(2,1)} %param.13) | copy-start | bytes 196612
  0.7 73.1 %copy-start.2 = (s32[1024]{0:T(1024)S(1)}, s32[1024]{0:T(1024)}, u32[]{:S(2)}) copy-start(s32[1024]{0:T(1024)} %param.17) | copy-start | bytes 12292
  0.7 73.1 %copy-start.3 = (f32[1024]{0:T(1024)S(1)}, f32[1024]{0:T(1024)}, u32[]{:S(2)}) copy-start(f32[1024]{0:T(1024)} %param.15) | copy-start | bytes 12292
  0.7 73.1 %copy-start.4 = (s32[100]{0:T(128)S(1)}, s32[100]{0:T(128)}, u32[]{:S(2)}) copy-start(s32[100]{0:T(128)} %occ_in.1) | copy-start | bytes 1204
  0.7 73.1 %copy-start.5 = (f32[100]{0:T(128)S(1)}, f32[100]{0:T(128)}, u32[]{:S(2)}) copy-start(f32[100]{0:T(128)} %eocc_in.1) | copy-start | bytes 1204
  0.7 73.1 %copy-start.6 = (s32[4]{0:T(128)S(1)}, s32[4]{0:T(128)}, u32[]{:S(2)}) copy-start(s32[4]{0:T(128)} %colo_in.1) | copy-start | bytes 52
